TPU v7x, 256 devices: a whole 4x4x8 slice. The times are simulated.
256 devices in a mesh: node: 64 (over x, z, core), local: 4 (over y).
Axes of the slice: x: 4, y: 4, z: 8, core: 2. Of those that a mesh axis runs over, the one named last changes fastest.
Arguments:
- grad_partials: bfloat16 [64, 460, 14848], P('node', None, 'local'), may hold values from -6 to 6
- old_master: float32 [64, 8, 14848], P('node', None, 'local'), may hold values from -6 to 6
- old_first: float32 [64, 8, 14848], P('node', None, 'local'), may hold values from -16 to 16
- old_second: float32 [64, 8, 14848], P('node', None, 'local'), may hold values from 1 to 100
- old_bounds: int32 [65], replicated, may hold values from 0 to 460, as said below
- new_bounds: int32 [53], replicated, may hold values from 0 to 460, as said below
- step_count: int32 [1], replicated, may hold values from 1 to 20
- learning_rate: float32 [1], replicated, may hold values from 0.05 to 0.4
Outputs:
- new_master: float32 [64, 12, 14848], P('node', None, 'local')
- new_first: float32 [64, 12, 14848], P('node', None, 'local')
- new_second: float32 [64, 12, 14848], P('node', None, 'local')
- secondary: bfloat16 [460, 14848], P('local')
Inputs may be any that keep to these rules, and one draw needn't show every extreme that they name: Increasing from 0 to 460, every entry a multiple of 4; each old owner holds 4 or 8 units, and some owner holds 8; slots of old_master, old_first and old_second past an owner's units belong to no unit. Between two successive entries of old_bounds and new_bounds taken together lie exactly 4 units, and no entry but the first and the last is in both, so one old owner hands at most 4 units to one new owner, and some pair hands exactly 4. `new_bounds`: increasing from 0 to 460, every entry a multiple of 4; each new owner holds 8 to 12 units, and some owner holds 12.
All inputs are finite; a program needn't handle non-finite values.
Results may differ from a plain program's by a relative error of at most 0.001.
Values may be sent and summed in bfloat16 or wider, within the bound.
A program may use at most 128 MiB of HBM per device.

v0:
```python
import jax
import jax.numpy as jnp
from jax import lax
from jax.sharding import PartitionSpec as P

SEG = 4


beta_first = 0.9
beta_second = 0.95
adam_eps = 1e-08
decay = 0.1


def owner_index(bounds, unit_ids):
    owners = bounds.shape[0] - 1
    return jnp.sum((bounds[None, 1:owners] <= unit_ids[:, None]).astype(jnp.int32), axis=1)


def adam_update(master, first, second, gradient, step_count, learning_rate):
    steps_taken = step_count[0].astype(jnp.float32)
    first_new = beta_first * first + (1.0 - beta_first) * gradient
    second_new = beta_second * second + (1.0 - beta_second) * gradient * gradient
    first_hat = first_new / (1.0 - jnp.power(jnp.float32(beta_first), steps_taken))
    second_hat = second_new / (1.0 - jnp.power(jnp.float32(beta_second), steps_taken))
    master_new = master - learning_rate[0] * (
        first_hat / (jnp.sqrt(second_hat) + adam_eps) + decay * master
    )
    return (master_new, first_new, second_new)


def reflected(ids, n_nodes):
    return (n_nodes // 2 - ids) % n_nodes


def layout_slots(bounds, capacity, n_nodes):
    owners = bounds.shape[0] - 1
    node_ids = jnp.arange(n_nodes)[:, None]
    owner_ids = reflected(node_ids, n_nodes)
    slot_ids = jnp.arange(capacity)[None, :]
    begin = bounds[jnp.minimum(owner_ids, owners)]
    finish = bounds[jnp.minimum(owner_ids + 1, owners)]
    unit_ids = begin + slot_ids
    usable = (owner_ids < owners) & (unit_ids < finish)
    return (unit_ids.reshape(-1), usable.reshape(-1))


def grad_term(grads, bounds, capacity, n_nodes):
    total_units = grads.shape[0]
    unit_flat, usable_flat = layout_slots(bounds, capacity, n_nodes)
    picked = jnp.take(grads, jnp.clip(unit_flat, 0, total_units - 1), axis=0).astype(jnp.float32)
    return jnp.where(usable_flat[:, None], picked, 0.0)


def on_device(
    grad_partials,
    old_master,
    old_first,
    old_second,
    old_bounds,
    new_bounds,
    step_count,
    learning_rate,
):
    n_nodes = lax.axis_size("node")
    node_rank = lax.axis_index("node")
    grads = grad_partials[0]
    total_units = grads.shape[0]
    cap_old = old_master.shape[1]
    columns = old_master.shape[2]
    new_count = new_bounds.shape[0] - 1
    cap_new = (2 + min(1, n_nodes - 1 - new_count)) * SEG
    old_state = (old_master[0], old_first[0], old_second[0])
    my_owner = reflected(node_rank, n_nodes)
    slot_ids = jnp.arange(cap_new)
    new_begin = new_bounds[jnp.minimum(my_owner, new_count)]
    new_finish = new_bounds[jnp.minimum(my_owner + 1, new_count)]
    wanted = new_begin + slot_ids
    wanted_ok = (my_owner < new_count) & (wanted < new_finish)
    wanted_clip = jnp.clip(wanted, 0, total_units - 1)
    wanted_owner = owner_index(old_bounds, wanted_clip)
    global_rows = wanted_owner * cap_old + (wanted_clip - old_bounds[wanted_owner])
    empty = jnp.zeros((cap_new, columns), jnp.float32)
    holding = (empty, empty, empty)
    pieces = (
        lax.all_gather(old_state[0], "node", axis=0, tiled=True),
        lax.all_gather(old_state[1], "node", axis=0, tiled=True),
        lax.all_gather(old_state[2], "node", axis=0, tiled=True),
    )
    length = pieces[0].shape[0]
    usable = wanted_ok & (global_rows >= 0) & (global_rows < length)
    clipped = jnp.clip(global_rows, 0, length - 1)
    moved = tuple(
        (
            jnp.where(usable[:, None], jnp.take(shard_rows, clipped, axis=0), current)
            for shard_rows, current in zip(pieces, holding)
        )
    )
    gradient = lax.psum_scatter(
        grad_term(grads, new_bounds, cap_new, n_nodes), "node", scatter_dimension=0, tiled=True
    )
    stepped = adam_update(moved[0], moved[1], moved[2], gradient, step_count, learning_rate)
    new_state = tuple((jnp.where(wanted_ok[:, None], member, 0.0) for member in stepped))
    source = new_state[0].astype(jnp.bfloat16)
    gathered = lax.all_gather(source, "node", axis=0, tiled=True)
    all_units = jnp.arange(total_units)
    owners = owner_index(new_bounds, all_units)
    holders = reflected(owners, n_nodes)
    row_ids = holders * cap_new + all_units - new_bounds[owners]
    ordered = jnp.take(gathered, row_ids, axis=0)
    secondary = lax.all_to_all(ordered, "local", split_axis=0, concat_axis=1, tiled=True)
    return (new_state[0][None], new_state[1][None], new_state[2][None], secondary)


def solution(mesh):
    return jax.shard_map(
        on_device,
        mesh=mesh,
        in_specs=(
            P("node", None, "local"),
            P("node", None, "local"),
            P("node", None, "local"),
            P("node", None, "local"),
            P(),
            P(),
            P(),
            P(),
        ),
        out_specs=(
            P("node", None, "local"),
            P("node", None, "local"),
            P("node", None, "local"),
            P("local", None),
        ),
        check_vma=False,
    )
```

profile of v0, /device:TPU:1, one launch (start us, length us, event | category | flops | bytes accessed | tf_op | source)
XLA Modules:
  0.0 556.5 jit_solution(1355914985867126475)
XLA Ops:
  13.0 5.6 gather_fusion.3
  18.5 9.8 %convert_select_fusion = f32[768,3712]{1,0:T(8,128)} fusion(bf16[768,3712]{1,0:T(8,128)(2,1)} %gather_fusion.3, pred[768]{0:T(1024)(128)(4,1)S(1)} %compare_and_fusion, pred[768]{0:T(1024)(128)(4,1)S(1)} %and.141), kind=kLoop, calls=%fused_computation.8 | loop fusion | flops 8552448 | bytes 17106432 | tf_op jit(solution)/shard_map/jit(_where)/select_n | solution.py:52
  28.4 171.4 %fusion = f32[16,3712]{1,0:T(8,128)S(1)} fusion(f32[768,3712]{1,0:T(8,128)} %convert_select_fusion), kind=kCustom, calls=%all-reduce-scatter | all-reduce-scatter fusion | flops 3801089 | bytes 11641856
  208.5 7.5 %collective-permute-done.15 = f32[12,3712]{1,0:T(8,128)S(1)} collective-permute-done((f32[12,3712]{1,0:T(8,128)S(1)}, f32[12,3712]{1,0:T(8,128)S(1)}, u32[]{:S(2)}, u32[]{:S(2)}) %collective-permute-start.15) | collective-permute-done | bytes 178208
  218.8 7.0 %collective-permute-start.14 = (f32[16,3712]{1,0:T(8,128)S(1)}, f32[16,3712]{1,0:T(8,128)S(1)}, u32[]{:S(2)}, u32[]{:S(2)}) collective-permute-start(f32[16,3712]{1,0:T(8,128)S(1)} %fusion), channel_id=1, source_target_pairs={{0,60},{4,64},{8,68},{12,72},{16,76},{20,80},{24,84},{28,88},{32,9... | collective-permute-start | bytes 712712
  225.8 9.9 %collective-permute-start.2 = (f32[16,3712]{1,0:T(8,128)S(1)}, f32[16,3712]{1,0:T(8,128)S(1)}, u32[]{:S(2)}, u32[]{:S(2)}) collective-permute-start(f32[16,3712]{1,0:T(8,128)S(1)} %fusion), channel_id=1, source_target_pairs={{0,12},{4,16},{8,20},{12,24},{16,28},{20,32},{24,36},{28,40},{32,4... | collective-permute-start | bytes 712712
  235.8 5.0 collective-permute-start.3
  247.8 5.7 %collective-permute-start.5 = (f32[16,3712]{1,0:T(8,128)S(1)}, f32[16,3712]{1,0:T(8,128)S(1)}, u32[]{:S(2)}, u32[]{:S(2)}) collective-permute-start(f32[16,3712]{1,0:T(8,128)S(1)} %fusion), channel_id=1, source_target_pairs={{0,24},{4,28},{8,32},{12,36},{16,40},{20,44},{24,48},{28,52},{32,5... | collective-permute-start | bytes 712712
  257.2 5.4 collective-permute-start.7
  267.9 6.7 %collective-permute-start.9 = (f32[16,3712]{1,0:T(8,128)S(1)}, f32[16,3712]{1,0:T(8,128)}, u32[]{:S(2)}, u32[]{:S(2)}) collective-permute-start(f32[16,3712]{1,0:T(8,128)S(1)} %fusion), channel_id=1, source_target_pairs={{0,40},{4,44},{8,48},{12,52},{16,56},{20,60},{24,64},{28,68},{32,7... | collective-permute-start | bytes 712712
  274.7 14.2 %collective-permute-done.5 = f32[16,3712]{1,0:T(8,128)S(1)} collective-permute-done((f32[16,3712]{1,0:T(8,128)S(1)}, f32[16,3712]{1,0:T(8,128)S(1)}, u32[]{:S(2)}, u32[]{:S(2)}) %collective-permute-start.5) | collective-permute-done | bytes 237600
  288.9 18.0 %collective-permute-done.6 = f32[16,3712]{1,0:T(8,128)S(1)} collective-permute-done((f32[16,3712]{1,0:T(8,128)S(1)}, f32[16,3712]{1,0:T(8,128)S(1)}, u32[]{:S(2)}, u32[]{:S(2)}) %collective-permute-start.6) | collective-permute-done | bytes 237600
  306.8 15.1 %collective-permute-done.7 = f32[16,3712]{1,0:T(8,128)S(1)} collective-permute-done((f32[16,3712]{1,0:T(8,128)S(1)}, f32[16,3712]{1,0:T(8,128)S(1)}, u32[]{:S(2)}, u32[]{:S(2)}) %collective-permute-start.7) | collective-permute-done | bytes 237600
  323.3 42.6 %concatenate = f32[268,3712]{1,0:T(8,128)} concatenate(f32[12,3712]{1,0:T(8,128)S(1)} %collective-permute-done.15, f32[16,3712]{1,0:T(8,128)S(1)} %collective-permute-done.14, f32[16,3712]{1,0:T(8,128)S(1)} %collective-permute-done.13, f32[16,3712]{1,0:T(8,128)S(1)} %collective-permute-done.12, f32[16,3712]{1,0:T(8,128)S(1)} %collective-permute-done.11, ...), dimensions={0} | concatenate | bytes 7958528
  369.8 3.8 gather_fusion.6
  373.7 3.8 gather_fusion.7
  381.4 4.4 compare_select_fusion.6
  386.2 28.8 %select_select_fusion.3 = s32[460]{0:T(512)S(1)} fusion(pred[460]{0:T(512)(128)(4,1)S(1)} %get-tuple-element.70, pred[460]{0:T(512)(128)(4,1)S(1)} %get-tuple-element.69, pred[460]{0:T(512)(128)(4,1)S(1)} %get-tuple-element.68, pred[460]{0:T(512)(128)(4,1)S(1)} %get-tuple-element.67, pred[460]{0:T(512)(128)(4,1)S(1)} %get-tuple-element.66, ...), kind=kLoop, calls=%fused_computation.116 | loop fusion | flops 21160 | bytes 25024 | tf_op jit(solution)/shard_map/gather | solution.py:109
  415.2 53.8 %all-gather.15.cloned.1.call-done = bf16[64,12,3712]{2,1,0:T(8,128)(2,1)} async-done(((bf16[1,12,3712]{2,1,0:T(8,128)(2,1)}), bf16[64,12,3712]{2,1,0:T(8,128)(2,1)}) %all-gather.15.cloned.1.call-update) | async-done | bytes 5701648 | tf_op jit(solution)/shard_map/all_gather | solution.py:105
  469.0 9.5 %reshape.577 = bf16[768,3712]{1,0:T(8,128)(2,1)} reshape(bf16[64,12,3712]{2,1,0:T(8,128)(2,1)} %all-gather.15.cloned.1.call-done) | data formatting | bytes 11403264
  478.5 10.6 %gather_fusion.4 = bf16[460,3712]{1,0:T(8,128)(2,1)S(1)} fusion(bf16[768,3712]{1,0:T(8,128)(2,1)} %reshape.577, s32[1024]{0:T(1024)S(1)} %pad_clamp_fusion), kind=kCustom, calls=%fused_computation.7 | custom fusion | bytes 6831920 | tf_op jit(solution)/shard_map/jit(_take)/gather | solution.py:110
  491.8 4.3 broadcast_select_fusion
  496.1 5.1 all-to-all-start
  503.8 39.2 %all-to-all-done = bf16[4,115,3712]{2,1,0:T(8,128)(2,1)} async-done(((bf16[4,115,3712]{2,1,0:T(8,128)(2,1)}), bf16[4,115,3712]{2,1,0:T(8,128)(2,1)}, u32[]{:S(2)}, u32[]{:S(2)}) %all-to-all-start) | async-done | bytes 3415072 | tf_op jit(solution)/shard_map/all_to_all | solution.py:111
  (100 shorter events, 52.9 us)
Async XLA Ops:
  7.2 358.7 %all-gather.9.cloned.1.call-start = ((), (), s32[]{:S(2)}) async-start(), calls=%async_computation.1 | async-start | bytes 7720960 | tf_op jit(solution)/shard_map/all_gather | solution.py:86
  7.9 361.8 %all-gather.11.cloned.1.call-start = ((), (), s32[]{:S(2)}) async-start(), calls=%async_computation.2 | async-start | bytes 7720960 | tf_op jit(solution)/shard_map/all_gather | solution.py:87
  8.7 365.0 %all-gather.13.cloned.1.call-start = ((), (), s32[]{:S(2)}) async-start(), calls=%async_computation.3 | async-start | bytes 7720960 | tf_op jit(solution)/shard_map/all_gather | solution.py:88
  9.4 459.6 %all-gather.15.cloned.1.call-start = ((), (), s32[]{:S(2)}) async-start(), calls=%async_computation.4 | async-start | bytes 7720960 | tf_op jit(solution)/shard_map/all_gather | solution.py:105
  28.4 178.6 %copy-start.3 = (s32[65]{0:T(128)S(1)}, s32[65]{0:T(128)}, u32[]{:S(2)}) copy-start(s32[65]{0:T(128)} %param.14) | copy-start | bytes 784
  28.4 178.7 %copy-start.2 = (s32[53]{0:T(128)S(1)}, s32[53]{0:T(128)}, u32[]{:S(2)}) copy-start(s32[53]{0:T(128)} %param.15) | copy-start | bytes 640
  28.4 216.8 %copy-start.9 = (u32[256]{0:T(256)S(1)}, u32[256]{0:T(256)}, u32[]{:S(2)}) copy-start(u32[256]{0:T(256)} %constant.191) | copy-start | bytes 3076
  199.8 17.7 %collective-permute-start = (f32[16,3712]{1,0:T(8,128)S(1)}, f32[16,3712]{1,0:T(8,128)S(1)}, u32[]{:S(2)}, u32[]{:S(2)}) collective-permute-start(f32[16,3712]{1,0:T(8,128)S(1)} %fusion), channel_id=1, source_target_pairs={{0,4},{4,8},{8,12},{12,16},{16,20},{20,24},{24,28},{28,32},{32,36}... | collective-permute-start | bytes 712712
  201.7 17.1 %collective-permute-start.1 = (f32[16,3712]{1,0:T(8,128)S(1)}, f32[16,3712]{1,0:T(8,128)S(1)}, u32[]{:S(2)}, u32[]{:S(2)}) collective-permute-start(f32[16,3712]{1,0:T(8,128)S(1)} %fusion), channel_id=1, source_target_pairs={{0,8},{4,12},{8,16},{12,20},{16,24},{20,28},{24,32},{28,36},{32,40... | collective-permute-start | bytes 712712
  203.0 22.8 %collective-permute-start.10 = (f32[16,3712]{1,0:T(8,128)S(1)}, f32[16,3712]{1,0:T(8,128)S(1)}, u32[]{:S(2)}, u32[]{:S(2)}) collective-permute-start(f32[16,3712]{1,0:T(8,128)S(1)} %fusion), channel_id=1, source_target_pairs={{0,44},{4,48},{8,52},{12,56},{16,60},{20,64},{24,68},{28,72},{32,7... | collective-permute-start | bytes 712712
  204.3 31.5 %collective-permute-start.11 = (f32[16,3712]{1,0:T(8,128)S(1)}, f32[16,3712]{1,0:T(8,128)S(1)}, u32[]{:S(2)}, u32[]{:S(2)}) collective-permute-start(f32[16,3712]{1,0:T(8,128)S(1)} %fusion), channel_id=1, source_target_pairs={{0,48},{4,52},{8,56},{12,60},{16,64},{20,68},{24,72},{28,76},{32,8... | collective-permute-start | bytes 712712
  205.7 10.3 %collective-permute-start.15 = (f32[12,3712]{1,0:T(8,128)S(1)}, f32[12,3712]{1,0:T(8,128)S(1)}, u32[]{:S(2)}, u32[]{:S(2)}) collective-permute-start(f32[12,3712]{1,0:T(8,128)S(1)} %slice.78), channel_id=1, source_target_pairs={{0,64},{4,68},{8,72},{12,76},{16,80},{20,84},{24,88},{28,92},{32,9... | collective-permute-start | bytes 534536
  216.0 24.9 %collective-permute-start.12 = (f32[16,3712]{1,0:T(8,128)S(1)}, f32[16,3712]{1,0:T(8,128)S(1)}, u32[]{:S(2)}, u32[]{:S(2)}) collective-permute-start(f32[16,3712]{1,0:T(8,128)S(1)} %fusion), channel_id=1, source_target_pairs={{0,52},{4,56},{8,60},{12,64},{16,68},{20,72},{24,76},{28,80},{32,8... | collective-permute-start | bytes 712712
  217.5 30.4 %collective-permute-start.13 = (f32[16,3712]{1,0:T(8,128)S(1)}, f32[16,3712]{1,0:T(8,128)S(1)}, u32[]{:S(2)}, u32[]{:S(2)}) collective-permute-start(f32[16,3712]{1,0:T(8,128)S(1)} %fusion), channel_id=1, source_target_pairs={{0,56},{4,60},{8,64},{12,68},{16,72},{20,76},{24,80},{28,84},{32,8... | collective-permute-start | bytes 712712
  218.8 34.8 %collective-permute-start.14 = (f32[16,3712]{1,0:T(8,128)S(1)}, f32[16,3712]{1,0:T(8,128)S(1)}, u32[]{:S(2)}, u32[]{:S(2)}) collective-permute-start(f32[16,3712]{1,0:T(8,128)S(1)} %fusion), channel_id=1, source_target_pairs={{0,60},{4,64},{8,68},{12,72},{16,76},{20,80},{24,84},{28,88},{32,9... | collective-permute-start | bytes 712712
  225.8 31.3 %collective-permute-start.2 = (f32[16,3712]{1,0:T(8,128)S(1)}, f32[16,3712]{1,0:T(8,128)S(1)}, u32[]{:S(2)}, u32[]{:S(2)}) collective-permute-start(f32[16,3712]{1,0:T(8,128)S(1)} %fusion), channel_id=1, source_target_pairs={{0,12},{4,16},{8,20},{12,24},{16,28},{20,32},{24,36},{28,40},{32,4... | collective-permute-start | bytes 712712
  235.8 26.7 %collective-permute-start.3 = (f32[16,3712]{1,0:T(8,128)S(1)}, f32[16,3712]{1,0:T(8,128)S(1)}, u32[]{:S(2)}, u32[]{:S(2)}) collective-permute-start(f32[16,3712]{1,0:T(8,128)S(1)} %fusion), channel_id=1, source_target_pairs={{0,16},{4,20},{8,24},{12,28},{16,32},{20,36},{24,40},{28,44},{32,4... | collective-permute-start | bytes 712712
  240.8 27.1 %collective-permute-start.4 = (f32[16,3712]{1,0:T(8,128)S(1)}, f32[16,3712]{1,0:T(8,128)S(1)}, u32[]{:S(2)}, u32[]{:S(2)}) collective-permute-start(f32[16,3712]{1,0:T(8,128)S(1)} %fusion), channel_id=1, source_target_pairs={{0,20},{4,24},{8,28},{12,32},{16,36},{20,40},{24,44},{28,48},{32,5... | collective-permute-start | bytes 712712
  247.8 41.0 %collective-permute-start.5 = (f32[16,3712]{1,0:T(8,128)S(1)}, f32[16,3712]{1,0:T(8,128)S(1)}, u32[]{:S(2)}, u32[]{:S(2)}) collective-permute-start(f32[16,3712]{1,0:T(8,128)S(1)} %fusion), channel_id=1, source_target_pairs={{0,24},{4,28},{8,32},{12,36},{16,40},{20,44},{24,48},{28,52},{32,5... | collective-permute-start | bytes 712712
  253.6 53.3 %collective-permute-start.6 = (f32[16,3712]{1,0:T(8,128)S(1)}, f32[16,3712]{1,0:T(8,128)S(1)}, u32[]{:S(2)}, u32[]{:S(2)}) collective-permute-start(f32[16,3712]{1,0:T(8,128)S(1)} %fusion), channel_id=1, source_target_pairs={{0,28},{4,32},{8,36},{12,40},{16,44},{20,48},{24,52},{28,56},{32,6... | collective-permute-start | bytes 712712
  257.2 64.7 %collective-permute-start.7 = (f32[16,3712]{1,0:T(8,128)S(1)}, f32[16,3712]{1,0:T(8,128)S(1)}, u32[]{:S(2)}, u32[]{:S(2)}) collective-permute-start(f32[16,3712]{1,0:T(8,128)S(1)} %fusion), channel_id=1, source_target_pairs={{0,32},{4,36},{8,40},{12,44},{16,48},{20,52},{24,56},{28,60},{32,6... | collective-permute-start | bytes 712712
  262.5 59.4 %collective-permute-start.8 = (f32[16,3712]{1,0:T(8,128)S(1)}, f32[16,3712]{1,0:T(8,128)S(1)}, u32[]{:S(2)}, u32[]{:S(2)}) collective-permute-start(f32[16,3712]{1,0:T(8,128)S(1)} %fusion), channel_id=1, source_target_pairs={{0,36},{4,40},{8,44},{12,48},{16,52},{20,56},{24,60},{28,64},{32,6... | collective-permute-start | bytes 712712
  267.9 55.4 %collective-permute-start.9 = (f32[16,3712]{1,0:T(8,128)S(1)}, f32[16,3712]{1,0:T(8,128)}, u32[]{:S(2)}, u32[]{:S(2)}) collective-permute-start(f32[16,3712]{1,0:T(8,128)S(1)} %fusion), channel_id=1, source_target_pairs={{0,40},{4,44},{8,48},{12,52},{16,56},{20,60},{24,64},{28,68},{32,7... | collective-permute-start | bytes 712712
  496.1 46.9 %all-to-all-start = ((bf16[4,115,3712]{2,1,0:T(8,128)(2,1)}), bf16[4,115,3712]{2,1,0:T(8,128)(2,1)}, u32[]{:S(2)}, u32[]{:S(2)}) async-start(bf16[4,115,3712]{2,1,0:T(8,128)(2,1)} %broadcast_select_fusion), calls=%async_computation | async-start | bytes 7127040 | tf_op jit(solution)/shard_map/all_to_all | solution.py:111
  (7 other events, 40.7 us)
Sparse Core Ops, SparseCore 0:
  10.7 96.5 all-gather.8
  110.0 86.2 all-gather.10
  199.0 132.6 all-gather.12
  379.9 89.0 all-gather.14
where the time goes:
time: 559 us; the launch traced here: 557 us
  blocking collectives  171 us (31%)
  waiting for transfers between devices  152 us (27%)
  local copies, waits for them, and re-layouts  100 us (18%)
  starting transfers between devices  63.7 us (11%)
  other arithmetic  52.5 us (9%)
  between operations  16.4 us (3%)
    unnamed x1, blocking collectives  171 us
    unnamed x29, local copies, waits for them, and re-layouts  60.3 us
    unnamed x20, waiting for transfers between devices  59 us
    unnamed x16, starting transfers between devices  58.5 us
    all_gather x1, waiting for transfers between devices, on_device(): gathered = lax.all_gather(source, 'node', axis=0, tiled=True)  53.8 us
    all_to_all x1, waiting for transfers between devices, on_device(): lax.all_to_all(ordered, 'local', split_axis=0, concat_axis=1, tiled=True)  39.2 us
    gather x3, other arithmetic, on_device(): row_ids = holders * cap_new + all_units - new_bounds[owners]  33.5 us
    gather x2, local copies, waits for them, and re-layouts, on_device(): ordered = jnp.take(gathered, row_ids, axis=0)  13.3 us
  transfers between devices with their start and end apart: 21, of which 7 were waited for; matrix products, arithmetic and copies ran while one was open for 51% of the time, Pallas kernels for 0%

commit v1 on v0

v1 whole, which is shorter than its diff:
```python
import jax
import jax.numpy as jnp
from jax import lax
from jax.experimental import pallas as pl
from jax.experimental.pallas import tpu as pltpu
from jax.sharding import PartitionSpec as P

MESH = pl.DeviceIdType.MESH
F32, BF16, I16, I32 = jnp.float32, jnp.bfloat16, jnp.int16, jnp.int32

UNITS = 460
WIDTH = 3712
LANE = 128
TILES = WIDTH // LANE
NODES = 64
CHIPS = 32
NX, NZ, NY = 4, 8, 4
HALF = 240
SECOND = 224
CHUNKS, ROWS = 3, 80
SEGMENTS = 115
CAP_NEW = 12
OWNERS = 52
PART = 64
LEVEL = 32760.0

beta_first = 0.9
beta_second = 0.95
adam_eps = 1e-08
decay = 0.1


def power(base, steps):
    result = jnp.float32(1.0)
    factor = float(base)
    for bit in range(5):
        result = jnp.where((steps // (1 << bit)) % 2 == 1, result * jnp.float32(factor), result)
        factor = factor * factor
    return result


def encode(value, inverse):
    return jnp.round(value * inverse).astype(I32).astype(I16)


def decode(code, scale):
    return code.astype(I32).astype(F32) * scale


def kernel(
    ob, nb, step_count, learning_rate, g, om, of, os_,
    o_m, o_f, o_s, o_w,
    gb, raw, summed, xsnd, xscl, xr, xs, zsum, zsnd, zscl, zr, zs, both,
    stg, st, mat, new, wb, blocks, snd, r2,
    raw_s, raw_r, xd_s, xd_r, xc_s, xc_r, zd_s, zd_r, zc_s, zc_r, gc_s, gc_r,
    s1_s, s1_r, st_s, st_r, w1_s, w1_r, w2_s, w2_r, rt_s, rt_r, lf_s, lf_r,
    rr_s, rr_r, rl_s, rl_r, cx_s, cx_r, s2_s, s2_r,
):
    node, y = lax.axis_index("node"), lax.axis_index("local")
    c, chip = node % 2, node // 2
    x, z = chip // NZ, chip % NZ

    def send(src, dst, ss, rs, to_chip, to_core=None, to_y=None):
        core = c if to_core is None else to_core
        return pltpu.make_async_remote_copy(
            src_ref=src, dst_ref=dst, send_sem=ss, recv_sem=rs,
            device_id=(to_chip * 2 + core, y if to_y is None else to_y), device_id_type=MESH,
        )

    sent = []

    def start(copy):
        copy.start()
        sent.append(copy)
        return copy

    barrier = pltpu.get_barrier_semaphore()

    def greet(d, carry):
        pl.semaphore_signal(barrier, inc=1, device_id=(((chip + d) % CHIPS) * 2 + c, y), device_id_type=MESH)
        return carry

    lax.fori_loop(1, CHIPS, greet, 0)
    pl.semaphore_signal(barrier, inc=1, device_id=(chip * 2 + 1 - c, y), device_id_type=MESH)
    for d in range(1, NY):
        pl.semaphore_signal(barrier, inc=1, device_id=(node, (y + d) % NY), device_id_type=MESH)

    def stage(t, carry):
        col = pl.ds(pl.multiple_of(t * LANE, LANE), LANE)
        gb[t, 0:448] = g[0, 0:448, col]
        gb[t, 448:464] = jnp.zeros((16, LANE), BF16)
        gb[t, 448:460] = g[0, 448:460, col]
        stg[t, 0] = om[0, :, col]
        stg[t, 1] = of[0, :, col]
        stg[t, 2] = os_[0, :, col]
        return carry

    lax.fori_loop(0, TILES, stage, 0)
    for t in range(TILES, CHIPS):
        stg[t] = jnp.zeros((3, 8, LANE), F32)
        xsnd[3, :, t - 24] = jnp.zeros((CHUNKS, ROWS, LANE), I16)

    pl.semaphore_wait(barrier, CHIPS - 1 + 1 + NY - 1)

    base, other = c * SECOND, (1 - c) * SECOND
    raws = []
    for k in range(CHUNKS):
        rows = pl.ds(pl.multiple_of(other + ROWS * k, 16), ROWS)
        raws.append(start(send(gb.at[:, rows], raw.at[k], raw_s.at[k], raw_r.at[k], chip, 1 - c)))

    def state_out(d, carry):
        to = (chip + d) % CHIPS
        send(stg.at[to], st.at[c, chip], s1_s, s1_r, to).start()
        return carry

    lax.fori_loop(1, CHIPS, state_out, 0)
    pltpu.make_async_copy(stg.at[chip], st.at[c, chip], s1_r).start()

    xcopies = []
    for k in range(CHUNKS):
        raws[k].wait_recv()
        rows = pl.ds(pl.multiple_of(base + ROWS * k, 16), ROWS)

        def add(t, top):
            value = gb[t, rows].astype(F32) + raw[k, t].astype(F32)
            summed[t] = value
            return jnp.maximum(top, jnp.abs(value))

        top = lax.fori_loop(0, TILES, add, jnp.zeros((ROWS, LANE), F32))
        top = jnp.maximum(jnp.max(top, axis=0, keepdims=True), 1e-30)
        xscl[k] = top / LEVEL
        inverse = LEVEL / top

        def code(t, carry):
            xsnd[t // NZ, k, t % NZ] = encode(summed[t], inverse)
            return carry

        lax.fori_loop(0, TILES, code, 0)
        for d in range(1, NX):
            gx = (x + d) % NX
            to = gx * NZ + z
            xcopies.append((
                start(send(xsnd.at[gx, k], xr.at[d - 1, k], xd_s.at[d - 1, k], xd_r.at[d - 1, k], to)),
                start(send(xscl.at[k], xs.at[d - 1, k], xc_s.at[d - 1, k], xc_r.at[d - 1, k], to)),
            ))

    zcopies = []
    for k in range(CHUNKS):
        for pair in xcopies[3 * k : 3 * k + 3]:
            pair[0].wait_recv()
            pair[1].wait_recv()

        def add_x(t, top):
            value = decode(xsnd[x, k, t], xscl[k])
            for d in range(NX - 1):
                value = value + decode(xr[d, k, t], xs[d, k])
            zsum[k, t] = value
            return jnp.maximum(top, jnp.abs(value))

        top = lax.fori_loop(0, NZ, add_x, jnp.zeros((ROWS, LANE), F32))
        top = jnp.maximum(jnp.max(top, axis=0, keepdims=True), 1e-30)
        zscl[k] = top / LEVEL
        inverse = LEVEL / top

        def code_z(t, carry):
            zsnd[k, t] = encode(zsum[k, t], inverse)
            return carry

        lax.fori_loop(0, NZ, code_z, 0)
        for d in range(1, NZ):
            gz = (z + d) % NZ
            to = x * NZ + gz
            zcopies.append((
                start(send(zsnd.at[k, gz], zr.at[d - 1, k], zd_s.at[d - 1, k], zd_r.at[d - 1, k], to)),
                start(send(zscl.at[k], zs.at[d - 1, k], zc_s.at[d - 1, k], zc_r.at[d - 1, k], to)),
            ))

    pltpu.make_async_copy(st.at[c], st.at[c], s1_r).wait()
    st_copy = start(send(st.at[c], st.at[c], st_s, st_r, chip, 1 - c))

    gcopies = []
    for k in range(CHUNKS):
        for pair in zcopies[7 * k : 7 * k + 7]:
            pair[0].wait_recv()
            pair[1].wait_recv()
        value = zsum[k, z]
        for d in range(NZ - 1):
            value = value + decode(zr[d, k], zs[d, k])
        rows = pl.ds(ROWS * k, ROWS)
        both[c, rows] = value
        gcopies.append(start(send(both.at[c, rows], both.at[c, rows], gc_s.at[k], gc_r.at[k], chip, 1 - c)))

    st_copy.wait_recv()
    for a in range(3):
        mat[a, 456:480] = jnp.zeros((24, LANE), F32)
        new[a, 464:480] = jnp.zeros((16, LANE), F32)

    def place(s, i):
        i = jnp.minimum(i + (ob[i + 1] <= 4 * s).astype(I32), NODES - 1)
        offset = jnp.clip(4 * s - ob[i], 0, 4)
        for a in range(3):
            mat[a, pl.ds(4 * s, 4)] = st[i % 2, i // 2, a, pl.ds(offset, 4)]
        return i

    lax.fori_loop(0, SEGMENTS, place, jnp.int32(0))

    for copy in gcopies:
        copy.wait_recv()

    steps = step_count[0]
    rate = learning_rate[0]
    first_left = 1.0 - power(beta_first, steps)
    second_left = 1.0 - power(beta_second, steps)

    def step(half, shift):
        def body(b, carry):
            rows = pl.ds(pl.multiple_of(b * 8, 8), 8)
            gradient = both[half, pl.ds(pl.multiple_of(b * 8 - shift, 8), 8)]
            master = mat[0, rows]
            first_new = beta_first * mat[1, rows] + (1.0 - beta_first) * gradient
            second_new = beta_second * mat[2, rows] + (1.0 - beta_second) * gradient * gradient
            first_hat = first_new / first_left
            second_hat = second_new / second_left
            new[0, rows] = master - rate * (first_hat / (jnp.sqrt(second_hat) + adam_eps) + decay * master)
            new[1, rows] = first_new
            new[2, rows] = second_new
            return carry

        return body

    lax.fori_loop(0, 29, step(0, 0), 0)
    lax.fori_loop(29, 58, step(1, SECOND), 0)

    for q in range(NY):
        wb[q] = new[0, 115 * q : 115 * q + 128].astype(BF16)
    mine = pl.ds(pl.multiple_of(c * PART, PART), PART)
    w1 = []
    for d in range(1, NY):
        to = (y + d) % NY
        w1.append(start(send(wb.at[to, mine], blocks.at[c, chip, y], w1_s.at[d - 1], w1_r.at[d - 1], chip, to_y=to)))
    blocks[c, chip, y] = wb[y, mine]

    def pick(m, carry):
        begin = jnp.clip(nb[2 * m + c], 0, UNITS)
        count = nb[2 * m + c + 1] - begin
        slot = lax.broadcasted_iota(I32, (CAP_NEW, LANE), 0)
        for a in range(3):
            rows = new[a, pl.ds(begin, CAP_NEW)]
            snd[m, CAP_NEW * a : CAP_NEW * (a + 1)] = jnp.where(slot < count, rows, 0.0)
        return carry

    lax.fori_loop(0, OWNERS // 2, pick, 0)

    for copy in w1:
        copy.wait_recv()
    w2 = []
    for d in range(1, NZ):
        to = x * NZ + (z + d) % NZ
        w2.append(start(send(blocks.at[c, chip], blocks.at[c, chip], w2_s.at[d - 1], w2_r.at[d - 1], to)))
    right, left = ((x + 1) % NX) * NZ, ((x + 3) % NX) * NZ
    across = ((x + 2) % NX) * NZ
    from_left, from_right = [], []

    def share(slot, e):
        start(send(blocks.at[c, slot], blocks.at[c, slot], cx_s.at[e], cx_r, chip, 1 - c))

    def spread(e):
        slot = x * NZ + (z + NZ - e) % NZ
        from_left.append(start(send(blocks.at[c, slot], blocks.at[c, slot], rt_s.at[e], rt_r.at[e], right + z)))
        from_right.append(start(send(blocks.at[c, slot], blocks.at[c, slot], lf_s.at[e], lf_r.at[e], left + z)))
        share(slot, e)

    spread(0)

    owner = (48 - c - chip) % CHIPS

    def owners_out(d, carry):
        to = (chip + d) % CHIPS
        m = (48 - c - to) % CHIPS

        @pl.when(m < OWNERS // 2)
        def _():
            send(snd.at[m], r2.at[chip], s2_s, s2_r, to).start()

        return carry

    lax.fori_loop(1, CHIPS, owners_out, 0)

    @pl.when(owner < OWNERS // 2)
    def _():
        pltpu.make_async_copy(snd.at[owner], r2.at[chip], s2_r).start()

    relay_left, relay_right = [], []

    def relay(e):
        at = (z + NZ - e) % NZ
        from_left[e].wait_recv()
        half = blocks.at[c, left + at, 0:2]
        relay_left.append(start(send(half, half, rr_s.at[e], rr_r.at[e], right + z)))
        share(left + at, 8 + e)
        from_right[e].wait_recv()
        half = blocks.at[c, right + at, 2:4]
        relay_right.append(start(send(half, half, rl_s.at[e], rl_r.at[e], left + z)))
        share(right + at, 16 + e)

    for e in range(1, NZ):
        w2[e - 1].wait_recv()
        spread(e)
        relay(e - 1)
    relay(NZ - 1)
    for e in range(NZ):
        relay_left[e].wait_recv()
        relay_right[e].wait_recv()
        share(across + (z + NZ - e) % NZ, 24 + e)

    @pl.when(owner < OWNERS // 2)
    def _():
        pltpu.make_async_copy(r2, r2, s2_r).wait()

        def fill(t, carry):
            col = pl.ds(pl.multiple_of(t * LANE, LANE), LANE)
            o_m[0, :, col] = r2[t, 0:12]
            o_f[0, :, col] = r2[t, 12:24]
            o_s[0, :, col] = r2[t, 24:36]
            return carry

        lax.fori_loop(0, TILES, fill, 0)
        pltpu.make_async_copy(snd.at[0:25], snd.at[0:25], s2_s).wait()

    @pl.when(owner >= OWNERS // 2)
    def _():
        for out in (o_m, o_f, o_s):
            out[...] = jnp.zeros_like(out)
        pltpu.make_async_copy(snd.at[0:26], snd.at[0:26], s2_s).wait()

    pltpu.make_async_copy(blocks.at[1 - c], blocks.at[1 - c], cx_r).wait()

    def finish(t, carry):
        for q in range(NY):
            col = pl.ds(pl.multiple_of(q * WIDTH + t * LANE, LANE), LANE)
            o_w[0:64, col] = blocks[0, t, q]
            o_w[64:115, col] = blocks[1, t, q, 0:51]
        return carry

    lax.fori_loop(0, TILES, finish, 0)

    pltpu.make_async_copy(stg.at[0:31], stg.at[0:31], s1_s).wait()
    for copy in sent:
        copy.wait_send()


def on_device(grad_partials, old_master, old_first, old_second, old_bounds, new_bounds, step_count, learning_rate):
    vmem, smem = pl.BlockSpec(memory_space=pltpu.VMEM), pl.BlockSpec(memory_space=pltpu.SMEM)
    dma = pltpu.SemaphoreType.DMA
    state = jax.ShapeDtypeStruct((1, CAP_NEW, WIDTH), F32)
    scratch = [
        pltpu.VMEM((TILES, 464, LANE), BF16),
        pltpu.VMEM((CHUNKS, TILES, ROWS, LANE), BF16),
        pltpu.VMEM((TILES, ROWS, LANE), F32),
        pltpu.VMEM((NX, CHUNKS, NZ, ROWS, LANE), I16),
        pltpu.VMEM((CHUNKS, 1, LANE), F32),
        pltpu.VMEM((NX - 1, CHUNKS, NZ, ROWS, LANE), I16),
        pltpu.VMEM((NX - 1, CHUNKS, 1, LANE), F32),
        pltpu.VMEM((CHUNKS, NZ, ROWS, LANE), F32),
        pltpu.VMEM((CHUNKS, NZ, ROWS, LANE), I16),
        pltpu.VMEM((CHUNKS, 1, LANE), F32),
        pltpu.VMEM((NZ - 1, CHUNKS, ROWS, LANE), I16),
        pltpu.VMEM((NZ - 1, CHUNKS, 1, LANE), F32),
        pltpu.VMEM((2, HALF, LANE), F32),
        pltpu.VMEM((CHIPS, 3, 8, LANE), F32),
        pltpu.VMEM((2, CHIPS, 3, 8, LANE), F32),
        pltpu.VMEM((3, 480, LANE), F32),
        pltpu.VMEM((3, 480, LANE), F32),
        pltpu.VMEM((NY, 128, LANE), BF16),
        pltpu.VMEM((2, CHIPS, NY, PART, LANE), BF16),
        pltpu.VMEM((OWNERS // 2, 40, LANE), F32),
        pltpu.VMEM((CHIPS, 40, LANE), F32),
        dma((CHUNKS,)), dma((CHUNKS,)),
        dma((NX - 1, CHUNKS)), dma((NX - 1, CHUNKS)),
        dma((NX - 1, CHUNKS)), dma((NX - 1, CHUNKS)),
        dma((NZ - 1, CHUNKS)), dma((NZ - 1, CHUNKS)),
        dma((NZ - 1, CHUNKS)), dma((NZ - 1, CHUNKS)),
        dma((CHUNKS,)), dma((CHUNKS,)),
        dma, dma,
        dma, dma,
        dma((NY - 1,)), dma((NY - 1,)),
        dma((NZ - 1,)), dma((NZ - 1,)),
        dma((NZ,)), dma((NZ,)),
        dma((NZ,)), dma((NZ,)),
        dma((NZ,)), dma((NZ,)),
        dma((NZ,)), dma((NZ,)),
        dma((CHIPS,)), dma,
        dma, dma,
    ]
    return pl.pallas_call(
        kernel,
        name="adamw_move",
        out_shape=(state, state, state, jax.ShapeDtypeStruct((115, 4 * WIDTH), BF16)),
        in_specs=[smem, smem, smem, smem, vmem, vmem, vmem, vmem],
        out_specs=(vmem, vmem, vmem, vmem),
        scratch_shapes=scratch,
        compiler_params=pltpu.CompilerParams(collective_id=0, has_side_effects=True, vmem_limit_bytes=56 * 2**20),
    )(old_bounds, new_bounds, step_count, learning_rate, grad_partials, old_master, old_first, old_second)


def solution(mesh):
    split = P("node", None, "local")
    return jax.shard_map(
        on_device,
        mesh=mesh,
        in_specs=(split, split, split, split, P(), P(), P(), P()),
        out_specs=(split, split, split, P("local", None)),
        check_vma=False,
    )
```

time: 559 us -> 110 us (0.20)
  blocking collectives: 171 us -> 0 us
  waiting for transfers between devices: 152 us -> 0 us
  Pallas kernels: 0 us -> 98.6 us
  local copies, waits for them, and re-layouts: 100 us -> 9.42 us
  starting transfers between devices: 63.7 us -> 0 us
  other arithmetic: 52.5 us -> 0 us
  between operations: 16.4 us -> 1.93 us
    unnamed x1 -> x0, blocking collectives: 171 us -> none
    pallas_call x0 -> x1, Pallas kernels: none -> 98.6 us  [on_device(): pl.pallas_call(kernel, name='adamw_move', out_shape=(state, state, state,...]
    unnamed x20 -> x0, waiting for transfers between devices: 59 us -> none
    unnamed x16 -> x0, starting transfers between devices: 58.5 us -> none
    unnamed x29 -> x1, local copies, waits for them, and re-layouts: 60.3 us -> 4.04 us
    all_gather x4 -> x0, waiting for transfers between devices: 53.9 us -> none  [the longest x1 53.8 us: on_device(): gathered = lax.all_gather(source, 'node', axis=0, tiled=True)]
    all_to_all x1 -> x0, waiting for transfers between devices: 39.2 us -> none  [on_device(): lax.all_to_all(ordered, 'local', split_axis=0, concat_axis=1, tiled=True)]
    gather x13 -> x0, local copies, waits for them, and re-layouts: 36.1 us -> none  [the longest x2 13.3 us: on_device(): ordered = jnp.take(gathered, row_ids, axis=0)]
  transfers between devices with their start and end apart: 21 -> 0, of which waited for: 7 -> 0; matrix products, arithmetic and copies ran while one was open for 51% -> 0% of each run, Pallas kernels for 0% -> 0%
where the time goes in v1:
time: 110 us
  Pallas kernels  98.6 us (90%)
  local copies, waits for them, and re-layouts  9.42 us (9%)
  between operations  1.93 us (2%)
    pallas_call x1, Pallas kernels, on_device(): pl.pallas_call(kernel, name='adamw_move', out_shape=(state, state, state,...  98.6 us
    pallas_call x3, local copies, waits for them, and re-layouts, on_device(): pl.pallas_call(kernel, name='adamw_move', out_shape=(state, state, state,...  5.39 us
    unnamed x1, local copies, waits for them, and re-layouts  4.04 us

profile of v1, /device:TPU:1, one launch (start us, length us, event | category | flops | bytes accessed | tf_op | source)
XLA Modules:
  0.0 109.9 jit_solution(3660375185123671045)
XLA Ops:
  1.9 98.6 %adamw_move.1 = (f32[1,12,3712]{2,1,0:T(8,128)}, f32[1,12,3712]{2,1,0:T(8,128)}, f32[1,12,3712]{2,1,0:T(8,128)}, bf16[115,14848]{1,0:T(8,128)(2,1)}) custom-call(s32[65]{0:T(128)} %ob.1, s32[53]{0:T(128)} %nb.1, s32[1]{0:T(128)S(6)} %copy.16.step_count, f32[1]{0:T(128)S(6)} %copy.17.learning_rate, bf16[1,460,3712]{2,1,0:T(8,128)(2,1)} %g.1, ...), custom_call_target="tpu_custom_call" | custom-call | tf_op jit(solution)/shard_map/adamw_move/pallas_call | solution.py:395
  100.5 1.8 %copy.12 = f32[1,12,3712]{2,0,1:T(1,128)} copy(f32[1,12,3712]{2,1,0:T(8,128)} %get-tuple-element.4) | data formatting | bytes 356352 | tf_op jit(solution)/shard_map/adamw_move/pallas_call | solution.py:395
  102.3 1.8 %copy.13 = f32[1,12,3712]{2,0,1:T(1,128)} copy(f32[1,12,3712]{2,1,0:T(8,128)} %get-tuple-element.5) | data formatting | bytes 356352 | tf_op jit(solution)/shard_map/adamw_move/pallas_call | solution.py:395
  104.1 1.8 %copy.14 = f32[1,12,3712]{2,0,1:T(1,128)} copy(f32[1,12,3712]{2,1,0:T(8,128)} %get-tuple-element.6) | data formatting | bytes 356352 | tf_op jit(solution)/shard_map/adamw_move/pallas_call | solution.py:395
  105.9 4.0 %copy.18 = bf16[115,14848]{1,0:T(8,128)(2,1)} copy(bf16[115,14848]{1,0:T(8,128)(2,1)} %get-tuple-element.15) | data formatting | bytes 6830080

commit v2 on v1

v2 whole, which is shorter than its diff:
```python
import jax
import jax.numpy as jnp
from jax import lax
from jax.experimental import pallas as pl
from jax.experimental.pallas import tpu as pltpu
from jax.sharding import PartitionSpec as P

MESH = pl.DeviceIdType.MESH
F32, BF16, I16, I32 = jnp.float32, jnp.bfloat16, jnp.int16, jnp.int32

UNITS = 460
WIDTH = 3712
LANE = 128
TILES = WIDTH // LANE
NODES = 64
CHIPS = 32
NX, NZ, NY = 4, 8, 4
HALF = 240
SECOND = 224
CHUNKS = ((0, 96), (96, 96), (192, 48))
NC = len(CHUNKS)
SEGMENTS = 115
CAP_NEW = 12
OWNERS = 52
PART = 64
LEVEL = 32760.0

beta_first = 0.9
beta_second = 0.95
adam_eps = 1e-08
decay = 0.1


def power(base, steps):
    result = jnp.float32(1.0)
    factor = float(base)
    for bit in range(5):
        result = jnp.where((steps // (1 << bit)) % 2 == 1, result * jnp.float32(factor), result)
        factor = factor * factor
    return result


def encode(value, inverse):
    return jnp.round(value * inverse).astype(I32).astype(I16)


def decode(code, scale):
    return code.astype(I32).astype(F32) * scale


def kernel(
    ob, nb, step_count, learning_rate, g, end, om, of, os_,
    blocks, r2,
    mine_g, raw, tail, olds, total, acode, right_code, left_code, scl, rscl, lscl,
    a_left, a_right, sa_left, sa_right, f_left, f_right, sf_left, sf_right,
    zsum, zsnd, zscl, zr, zs, both,
    stg, st, mat, new, wb, own, snd, zero,
    in_s, own_g, raw_s, raw_r, a_s, a_r, as_s, as_r, f_s, f_r, fs_s, fs_r, zd_s, zd_r, zc_s, zc_r, gc_s, gc_r,
    s1_s, s1_r, st_s, st_r, w1_s, w1_r, zu_s, zu_r, zd2_s, zd2_r, rt_s, rt_r, lf_s, lf_r,
    rr_s, rr_r, rl_s, rl_r, cx_s, cx_r, s2_s, s2_r, own_s,
):
    node, y = lax.axis_index("node"), lax.axis_index("local")
    c, chip = node % 2, node // 2
    x, z = chip // NZ, chip % NZ

    def send(src, dst, ss, rs, to_chip, to_core=None, to_y=None):
        core = c if to_core is None else to_core
        return pltpu.make_async_remote_copy(
            src_ref=src, dst_ref=dst, send_sem=ss, recv_sem=rs,
            device_id=(to_chip * 2 + core, y if to_y is None else to_y), device_id_type=MESH,
        )

    sent = []

    def start(copy):
        copy.start()
        sent.append(copy)
        return copy

    barrier = pltpu.get_barrier_semaphore()

    def greet(d, carry):
        pl.semaphore_signal(barrier, inc=1, device_id=(((chip + d) % CHIPS) * 2 + c, y), device_id_type=MESH)
        return carry

    lax.fori_loop(1, CHIPS, greet, 0)
    pl.semaphore_signal(barrier, inc=1, device_id=(chip * 2 + 1 - c, y), device_id_type=MESH)
    for d in range(1, NY):
        pl.semaphore_signal(barrier, inc=1, device_id=(node, (y + d) % NY), device_id_type=MESH)

    state_in = [pltpu.make_async_copy(old.at[0], olds.at[a], in_s.at[a]) for a, old in enumerate((om, of, os_))]
    for copy in state_in:
        copy.start()
    row = lax.broadcasted_iota(I32, (16, WIDTH), 0)
    tail[...] = jnp.where(row < 12, end[0].astype(F32), 0.0).astype(BF16)

    @pl.when(c == 0)
    def _():
        pltpu.make_async_copy(g.at[0, 0:HALF], mine_g, own_g).start()

    @pl.when(c == 1)
    def _():
        pltpu.make_async_copy(g.at[0, SECOND:448], mine_g.at[0:224], own_g).start()
        mine_g[224:240] = tail[...]

    for copy in state_in:
        copy.wait()

    def stage(t, carry):
        col = pl.ds(pl.multiple_of(t * LANE, LANE), LANE)
        for a in range(3):
            stg[t, a] = olds[a, :, col]
        return carry

    lax.fori_loop(0, TILES, stage, 0)
    for t in range(TILES, CHIPS):
        total[t] = jnp.zeros((HALF, LANE), F32)

    pl.semaphore_wait(barrier, CHIPS - 1 + 1 + NY - 1)

    @pl.when(c == 0)
    def _():
        for k, (first, rows) in enumerate(CHUNKS):
            rows = min(rows, 224 - first)
            send(g.at[0, SECOND + first : SECOND + first + rows], raw.at[first : first + rows], raw_s.at[k], raw_r.at[k], chip, 1).start()
        send(tail, raw.at[224:240], raw_s.at[NC - 1], raw_r.at[NC - 1], chip, 1).start()

    @pl.when(c == 1)
    def _():
        for k, (first, rows) in enumerate(CHUNKS):
            send(g.at[0, first : first + rows], raw.at[first : first + rows], raw_s.at[k], raw_r.at[k], chip, 0).start()

    @pl.when(c == 0)
    def _():
        pltpu.make_async_copy(mine_g, mine_g, own_g).wait()

    @pl.when(c == 1)
    def _():
        pltpu.make_async_copy(mine_g.at[0:224], mine_g.at[0:224], own_g).wait()

    def state_out(d, carry):
        to = (chip + d) % CHIPS

        @pl.when(to < TILES)
        def _():
            send(stg.at[to], st.at[c, chip], s1_s, s1_r, to).start()

        return carry

    lax.fori_loop(1, CHIPS, state_out, 0)

    @pl.when(chip < TILES)
    def _():
        pltpu.make_async_copy(stg.at[chip], st.at[c, chip], s1_r).start()

    right_x, left_x, far_x = (x + 1) % NX, (x + 3) % NX, (x + 2) % NX
    right_chip, left_chip = right_x * NZ + z, left_x * NZ + z
    acopies, fcopies, zcopies = [], [], []

    def pair(k):
        first, rows = CHUNKS[k]
        at = slice(first, first + rows)
        pltpu.make_async_copy(raw.at[at], raw.at[at], raw_r.at[k]).wait()

        def add(t, top):
            col = pl.ds(pl.multiple_of(t * LANE, LANE), LANE)
            value = mine_g[at, col].astype(F32) + raw[at, col].astype(F32)
            total[t, at] = value
            return jnp.maximum(top, jnp.abs(value))

        top = lax.fori_loop(0, TILES, add, jnp.zeros((rows, LANE), F32))
        top = jnp.maximum(jnp.max(top, axis=0, keepdims=True), 1e-30)
        scl[k] = top / LEVEL
        inverse = LEVEL / top

        def code(t, carry):
            acode[t, at] = encode(total[far_x * NZ + t, at], inverse)
            return carry

        lax.fori_loop(0, NZ, code, 0)
        acopies.append((
            start(send(acode.at[0:4, at], a_left.at[:, at], a_s.at[0, k], a_r.at[0, k], right_chip)),
            start(send(acode.at[4:8, at], a_right.at[:, at], a_s.at[1, k], a_r.at[1, k], left_chip)),
            start(send(scl.at[k], sa_left.at[k], as_s.at[0, k], as_r.at[0, k], right_chip)),
            start(send(scl.at[k], sa_right.at[k], as_s.at[1, k], as_r.at[1, k], left_chip)),
        ))

    def neighbours(k):
        first, rows = CHUNKS[k]
        at = slice(first, first + rows)
        for copy in acopies[k]:
            copy.wait_recv()
        rscl[k] = scl[k] + sa_left[k]
        lscl[k] = scl[k] + sa_right[k]
        to_right, to_left = 1.0 / rscl[k], 1.0 / lscl[k]

        def code(t, carry):
            through = decode(a_left[t, at], sa_left[k])
            right_code[t, at] = encode(total[right_x * NZ + t, at] + through, to_right)
            right_code[t + 4, at] = encode(total[right_x * NZ + t + 4, at], to_right)
            through = decode(a_right[t, at], sa_right[k])
            left_code[t, at] = encode(total[left_x * NZ + t, at], to_left)
            left_code[t + 4, at] = encode(total[left_x * NZ + t + 4, at] + through, to_left)
            return carry

        lax.fori_loop(0, 4, code, 0)
        fcopies.append((
            start(send(right_code.at[:, at], f_left.at[:, at], f_s.at[0, k], f_r.at[0, k], right_chip)),
            start(send(left_code.at[:, at], f_right.at[:, at], f_s.at[1, k], f_r.at[1, k], left_chip)),
            start(send(rscl.at[k], sf_left.at[k], fs_s.at[0, k], fs_r.at[0, k], right_chip)),
            start(send(lscl.at[k], sf_right.at[k], fs_s.at[1, k], fs_r.at[1, k], left_chip)),
        ))

    def along_z(k):
        first, rows = CHUNKS[k]
        at = slice(first, first + rows)
        for copy in fcopies[k]:
            copy.wait_recv()
        zscl[k] = scl[k] + sf_left[k] + sf_right[k]
        inverse = 1.0 / zscl[k]

        def code(t, carry):
            value = total[x * NZ + t, at] + decode(f_left[t, at], sf_left[k]) + decode(f_right[t, at], sf_right[k])
            zsum[t, at] = value
            zsnd[t, at] = encode(value, inverse)
            return carry

        lax.fori_loop(0, NZ, code, 0)
        for d in range(1, NZ):
            gz = (z + d) % NZ
            to = x * NZ + gz
            zcopies.append((
                start(send(zsnd.at[gz, at], zr.at[d - 1, at], zd_s.at[d - 1, k], zd_r.at[d - 1, k], to)),
                start(send(zscl.at[k], zs.at[d - 1, k], zc_s.at[d - 1, k], zc_r.at[d - 1, k], to)),
            ))

    pair(0)
    pair(1)
    neighbours(0)
    pair(2)
    neighbours(1)
    along_z(0)
    neighbours(2)

    @pl.when(chip < TILES)
    def _():
        pltpu.make_async_copy(st.at[c], st.at[c], s1_r).wait()

    st_copy = start(send(st.at[c], st.at[c], st_s, st_r, chip, 1 - c))
    along_z(1)

    st_copy.wait_recv()
    for a in range(3):
        mat[a, 456:480] = jnp.zeros((24, LANE), F32)
        new[a, 464:480] = jnp.zeros((16, LANE), F32)

    def place(s, i):
        i = jnp.minimum(i + (ob[i + 1] <= 4 * s).astype(I32), NODES - 1)
        offset = jnp.clip(4 * s - ob[i], 0, 4)
        for a in range(3):
            mat[a, pl.ds(4 * s, 4)] = st[i % 2, i // 2, a, pl.ds(offset, 4)]
        return i

    lax.fori_loop(0, SEGMENTS, place, jnp.int32(0))
    along_z(2)

    gcopies = []
    for k, (first, rows) in enumerate(CHUNKS):
        at = slice(first, first + rows)
        for pair_of in zcopies[7 * k : 7 * k + 7]:
            pair_of[0].wait_recv()
            pair_of[1].wait_recv()
        value = zsum[z, at]
        for d in range(NZ - 1):
            value = value + decode(zr[d, at], zs[d, k])
        both[c, at] = value
        gcopies.append(start(send(both.at[c, at], both.at[c, at], gc_s.at[k], gc_r.at[k], chip, 1 - c)))

    for copy in gcopies:
        copy.wait_recv()

    steps = step_count[0]
    rate = learning_rate[0]
    first_left = 1.0 - power(beta_first, steps)
    second_left = 1.0 - power(beta_second, steps)

    def step(half, begin, size):
        def body(b, carry):
            rows = pl.ds(pl.multiple_of(begin + b * size, 16), size)
            gradient = both[half, pl.ds(pl.multiple_of(b * size, 16), size)]
            master = mat[0, rows]
            first_new = beta_first * mat[1, rows] + (1.0 - beta_first) * gradient
            second_new = beta_second * mat[2, rows] + (1.0 - beta_second) * gradient * gradient
            first_hat = first_new / first_left
            second_hat = second_new / second_left
            new[0, rows] = master - rate * (first_hat / (jnp.sqrt(second_hat) + adam_eps) + decay * master)
            new[1, rows] = first_new
            new[2, rows] = second_new
            return carry

        return body

    lax.fori_loop(0, 7, step(0, 0, 32), 0)
    lax.fori_loop(0, 5, step(1, SECOND, 48), 0)

    for q in range(NY):
        wb[q] = new[0, 115 * q : 115 * q + 128].astype(BF16)
    mine = pl.ds(pl.multiple_of(c * PART, PART), PART)
    w1 = []
    for d in range(1, NY):
        to = (y + d) % NY
        w1.append(start(send(wb.at[to, mine], own.at[y], w1_s.at[d - 1], w1_r.at[d - 1], chip, to_y=to)))
    own[y] = wb[y, mine]

    def pick(m, carry):
        begin = jnp.clip(nb[2 * m + c], 0, UNITS)
        count = nb[2 * m + c + 1] - begin
        slot = lax.broadcasted_iota(I32, (CAP_NEW, LANE), 0)
        for a in range(3):
            rows = new[a, pl.ds(begin, CAP_NEW)]
            snd[m, CAP_NEW * a : CAP_NEW * (a + 1)] = jnp.where(slot < count, rows, 0.0)
        return carry

    lax.fori_loop(0, OWNERS // 2, pick, 0)

    for copy in w1:
        copy.wait_recv()
    keep = pltpu.make_async_copy(own, blocks.at[c, chip], own_s)
    keep.start()
    up, down = x * NZ + (z + 1) % NZ, x * NZ + (z + NZ - 1) % NZ
    right, left = ((x + 1) % NX) * NZ, ((x + 3) % NX) * NZ
    across = ((x + 2) % NX) * NZ
    from_left, from_right, relay_left, relay_right = [], [], [], []

    def share(src, slot, e):
        start(send(src, blocks.at[c, slot], cx_s.at[e], cx_r, chip, 1 - c))

    def climb(src, slot, s, part=None):
        dst = blocks.at[c, slot] if part is None else blocks.at[c, slot, part]
        return start(send(src, dst, zu_s.at[s], zu_r.at[s], up))

    def descend(src, slot, s, part=None):
        dst = blocks.at[c, slot] if part is None else blocks.at[c, slot, part]
        return start(send(src, dst, zd2_s.at[s], zd2_r.at[s], down))

    def spread(src, slot, e):
        from_left.append(start(send(src, blocks.at[c, slot], rt_s.at[e], rt_r.at[e], right + z)))
        from_right.append(start(send(src, blocks.at[c, slot], lf_s.at[e], lf_r.at[e], left + z)))
        share(src, slot, e)

    def relay(at, e):
        from_left[e].wait_recv()
        half = blocks.at[c, left + at, 0:2]
        relay_left.append(start(send(half, half, rr_s.at[e], rr_r.at[e], right + z)))
        share(blocks.at[c, left + at], left + at, 8 + e)
        from_right[e].wait_recv()
        half = blocks.at[c, right + at, 2:4]
        relay_right.append(start(send(half, half, rl_s.at[e], rl_r.at[e], left + z)))
        share(blocks.at[c, right + at], right + at, 16 + e)

    owner = (48 - c - chip) % CHIPS

    def owners_out(d, carry):
        to = (chip + d) % CHIPS
        m = (48 - c - to) % CHIPS

        @pl.when((m < OWNERS // 2) & (chip < TILES))
        def _():
            send(snd.at[m], r2.at[chip], s2_s, s2_r, to).start()

        return carry

    @pl.when((owner < OWNERS // 2) & (chip < TILES))
    def _():
        pltpu.make_async_copy(snd.at[owner], r2.at[chip], s2_r).start()

    place_of = [z]
    climbing, descending = climb(own, chip, 0), descend(own, chip, 0)
    spread(own, chip, 0)
    lax.fori_loop(1, 8, owners_out, 0)
    for s in range(1, NZ // 2):
        low, high = (z + NZ - s) % NZ, (z + s) % NZ
        climbing.wait_recv()
        block = blocks.at[c, x * NZ + low]
        if s < NZ // 2 - 1:
            climbing = climb(block, x * NZ + low, s)
        else:
            climbing = climb(blocks.at[c, x * NZ + low, 0:2], x * NZ + low, s, slice(0, 2))
        spread(block, x * NZ + low, 2 * s - 1)
        descending.wait_recv()
        block = blocks.at[c, x * NZ + high]
        if s < NZ // 2 - 1:
            descending = descend(block, x * NZ + high, s)
        else:
            descending = descend(blocks.at[c, x * NZ + high, 2:4], x * NZ + high, s, slice(2, 4))
        spread(block, x * NZ + high, 2 * s)
        for e in range(len(place_of) - (1 if s == 1 else 2), len(place_of)):
            relay(place_of[e], e)
        place_of += [low, high]
        lax.fori_loop(8 * s, 8 * s + 8, owners_out, 0)
    climbing.wait_recv()
    descending.wait_recv()
    last = (z + NZ // 2) % NZ
    spread(blocks.at[c, x * NZ + last], x * NZ + last, NZ - 1)
    place_of.append(last)

    for e in range(NZ - 3, NZ):
        relay(place_of[e], e)
    for e in range(NZ):
        relay_left[e].wait_recv()
        relay_right[e].wait_recv()
        slot = across + place_of[e]
        share(blocks.at[c, slot], slot, 24 + e)

    @pl.when(owner < OWNERS // 2)
    def _():
        pltpu.make_async_copy(r2.at[0:TILES], r2.at[0:TILES], s2_r).wait()

    @pl.when(owner >= OWNERS // 2)
    def _():
        zero[...] = jnp.zeros_like(zero)
        clear = pltpu.make_async_copy(zero, r2.at[0:TILES], s2_r)
        clear.start()
        clear.wait()

    @pl.when((owner < OWNERS // 2) & (chip < TILES))
    def _():
        pltpu.make_async_copy(snd.at[0:25], snd.at[0:25], s2_s).wait()

    @pl.when((owner >= OWNERS // 2) & (chip < TILES))
    def _():
        pltpu.make_async_copy(snd.at[0:26], snd.at[0:26], s2_s).wait()

    keep.wait()
    pltpu.make_async_copy(blocks.at[1 - c], blocks.at[1 - c], cx_r).wait()
    for k, (first, rows) in enumerate(CHUNKS):
        pltpu.make_async_copy(raw.at[first : first + rows], raw.at[first : first + rows], raw_s.at[k]).wait()

    @pl.when(chip < TILES)
    def _():
        pltpu.make_async_copy(stg.at[0:28], stg.at[0:28], s1_s).wait()

    @pl.when(chip >= TILES)
    def _():
        pltpu.make_async_copy(stg.at[0:29], stg.at[0:29], s1_s).wait()

    for copy in sent:
        copy.wait_send()


def lay_out(blocks, r2, o_m, o_f, o_s, o_w):
    q = pl.program_id(0)

    def tile(t, carry):
        for a, out in enumerate((o_m, o_f, o_s)):
            for s in range(CAP_NEW):
                out[s, t] = r2[t, CAP_NEW * a + s : CAP_NEW * a + s + 1]
        return carry

    lax.fori_loop(8 * q, jnp.minimum(8 * q + 8, TILES), tile, 0)
    for t in range(TILES):
        col = slice(t * LANE, (t + 1) * LANE)
        o_w[0:64, col] = blocks[0, t, 0]
        o_w[64:115, col] = blocks[1, t, 0, 0:51]


def on_device(grad_partials, old_master, old_first, old_second, old_bounds, new_bounds, step_count, learning_rate):
    smem = pl.BlockSpec(memory_space=pltpu.SMEM)
    dma = pltpu.SemaphoreType.DMA
    hbm = pl.BlockSpec(memory_space=pl.ANY)
    scale = pltpu.VMEM((NC, 1, LANE), F32)
    scratch = [
        pltpu.VMEM((HALF, WIDTH), BF16),
        pltpu.VMEM((HALF, WIDTH), BF16),
        pltpu.VMEM((16, WIDTH), BF16),
        pltpu.VMEM((3, 8, WIDTH), F32),
        pltpu.VMEM((CHIPS, HALF, LANE), F32),
        pltpu.VMEM((NZ, HALF, LANE), I16),
        pltpu.VMEM((NZ, HALF, LANE), I16),
        pltpu.VMEM((NZ, HALF, LANE), I16),
        scale, scale, scale,
        pltpu.VMEM((NZ // 2, HALF, LANE), I16),
        pltpu.VMEM((NZ // 2, HALF, LANE), I16),
        scale, scale,
        pltpu.VMEM((NZ, HALF, LANE), I16),
        pltpu.VMEM((NZ, HALF, LANE), I16),
        scale, scale,
        pltpu.VMEM((NZ, HALF, LANE), F32),
        pltpu.VMEM((NZ, HALF, LANE), I16),
        scale,
        pltpu.VMEM((NZ - 1, HALF, LANE), I16),
        pltpu.VMEM((NZ - 1, NC, 1, LANE), F32),
        pltpu.VMEM((2, HALF, LANE), F32),
        pltpu.VMEM((CHIPS, 3, 8, LANE), F32),
        pltpu.VMEM((2, CHIPS, 3, 8, LANE), F32),
        pltpu.VMEM((3, 480, LANE), F32),
        pltpu.VMEM((3, 480, LANE), F32),
        pltpu.VMEM((NY, 128, LANE), BF16),
        pltpu.VMEM((NY, PART, LANE), BF16),
        pltpu.VMEM((OWNERS // 2, 3 * CAP_NEW, LANE), F32),
        pltpu.VMEM((TILES, 3 * CAP_NEW, LANE), F32),
        dma((3,)), dma,
        dma((NC,)), dma((NC,)),
        dma((2, NC)), dma((2, NC)), dma((2, NC)), dma((2, NC)),
        dma((2, NC)), dma((2, NC)), dma((2, NC)), dma((2, NC)),
        dma((NZ - 1, NC)), dma((NZ - 1, NC)), dma((NZ - 1, NC)), dma((NZ - 1, NC)),
        dma((NC,)), dma((NC,)),
        dma, dma,
        dma, dma,
        dma((NY - 1,)), dma((NY - 1,)),
        dma((NZ // 2,)), dma((NZ // 2,)),
        dma((NZ // 2,)), dma((NZ // 2,)),
        dma((NZ,)), dma((NZ,)),
        dma((NZ,)), dma((NZ,)),
        dma((NZ,)), dma((NZ,)),
        dma((NZ,)), dma((NZ,)),
        dma((CHIPS,)), dma,
        dma, dma,
        dma,
    ]
    blocks, r2 = pl.pallas_call(
        kernel,
        name="adamw_move",
        out_shape=(
            jax.ShapeDtypeStruct((2, CHIPS, NY, PART, LANE), BF16),
            jax.ShapeDtypeStruct((CHIPS, 3 * CAP_NEW, LANE), F32),
        ),
        in_specs=[smem, smem, smem, smem, hbm, pl.BlockSpec((1, 16, WIDTH), lambda i: (0, 28, 0)), hbm, hbm, hbm],
        grid=(1,),
        out_specs=(hbm, hbm),
        scratch_shapes=scratch,
        compiler_params=pltpu.CompilerParams(collective_id=0, has_side_effects=True, vmem_limit_bytes=56 * 2**20),
    )(old_bounds, new_bounds, step_count, learning_rate, grad_partials, grad_partials, old_master, old_first, old_second)
    whole = pl.BlockSpec((CAP_NEW, TILES, 1, LANE), lambda q: (0, 0, 0, 0))
    rows = jax.ShapeDtypeStruct((CAP_NEW, TILES, 1, LANE), F32)
    outs = pl.pallas_call(
        lay_out,
        name="lay_out",
        grid=(NY,),
        out_shape=(rows, rows, rows, jax.ShapeDtypeStruct((115, NY * WIDTH), BF16)),
        in_specs=[
            pl.BlockSpec((2, CHIPS, 1, PART, LANE), lambda q: (0, 0, q, 0, 0)),
            pl.BlockSpec((CHIPS, 3 * CAP_NEW, LANE), lambda q: (0, 0, 0)),
        ],
        out_specs=(whole, whole, whole, pl.BlockSpec((115, WIDTH), lambda q: (0, q))),
    )(blocks, r2)
    return tuple(out.reshape(1, CAP_NEW, WIDTH) for out in outs[:3]) + (outs[3],)


def solution(mesh):
    split = P("node", None, "local")
    return jax.shard_map(
        on_device,
        mesh=mesh,
        in_specs=(split, split, split, split, P(), P(), P(), P()),
        out_specs=(split, split, split, P("local", None)),
        check_vma=False,
    )
```

time: 110 us -> 91 us (0.83)
  Pallas kernels: 98.6 us -> 88.8 us
  local copies, waits for them, and re-layouts: 9.42 us -> 0 us
    pallas_call x1 -> x2, Pallas kernels: 98.6 us -> 88.8 us  [the longest x1 83.5 us: on_device(): pl.pallas_call(kernel, name='adamw_move', out_shape=(jax.ShapeDtypeStruct...]
    pallas_call x3 -> x0, local copies, waits for them, and re-layouts: 5.39 us -> none  [on_device(): pl.pallas_call(kernel, name='adamw_move', out_shape=(state, state, state,...]
    unnamed x1 -> x0, local copies, waits for them, and re-layouts: 4.04 us -> none
where the time goes in v2:
time: 91 us; the launch traced here: 90.7 us
  Pallas kernels  88.8 us (98%)
  between operations  1.93 us (2%)
    pallas_call x1, Pallas kernels, on_device(): pl.pallas_call(kernel, name='adamw_move', out_shape=(jax.ShapeDtypeStruct...  83.5 us
    pallas_call x1, Pallas kernels, on_device(): pl.pallas_call(lay_out, name='lay_out', grid=(NY,), out_shape=(rows, rows...  5.33 us

profile of v2, /device:TPU:1, one launch (start us, length us, event | category | flops | bytes accessed | tf_op | source)
XLA Modules:
  0.0 90.7 jit_solution(13617739528199561412)
XLA Ops:
  1.9 83.5 %adamw_move.1 = (bf16[2,32,4,64,128]{4,3,2,1,0:T(8,128)(2,1)}, f32[32,36,128]{2,1,0:T(8,128)}) custom-call(s32[65]{0:T(128)} %ob.1, s32[53]{0:T(128)} %nb.1, s32[1]{0:T(128)S(6)} %copy.15.step_count, f32[1]{0:T(128)S(6)} %copy.16.learning_rate, bf16[1,460,3712]{2,1,0:T(8,128)(2,1)} %end.1, bf16[1,460,3712]{2,1,0:T(8,128)(2,1)} %end.1, f32[1,8,3712]{2,1,0:T(8,128)} %om.1, ...), custom_call_target="tpu_custom_call" | custom-call | tf_op jit(solution)/shard_map/adamw_move/pallas_call | solution.py:521
  85.4 5.3 %lay_out.1 = (f32[12,29,1,128]{3,2,1,0:T(1,128)}, f32[12,29,1,128]{3,2,1,0:T(1,128)}, f32[12,29,1,128]{3,2,1,0:T(1,128)}, bf16[115,14848]{1,0:T(8,128)(2,1)}) custom-call(bf16[2,32,4,64,128]{4,3,2,1,0:T(8,128)(2,1)} %get-tuple-element.10.blocks, f32[32,36,128]{2,1,0:T(8,128)} %get-tuple-element.11.r2), custom_call_target="tpu_custom_call" | custom-call | tf_op jit(solution)/shard_map/lay_out/pallas_call | solution.py:536

commit v3 on v2

--- a/solution.py
+++ b/solution.py
@@ -17,7 +17,7 @@
 NX, NZ, NY = 4, 8, 4
 HALF = 240
 SECOND = 224
-CHUNKS = ((0, 96), (96, 96), (192, 48))
+CHUNKS = ((0, 64), (64, 64), (128, 64), (192, 48))
 NC = len(CHUNKS)
 SEGMENTS = 115
 CAP_NEW = 12
@@ -49,14 +49,15 @@
 
 
 def kernel(
-    ob, nb, step_count, learning_rate, g, end, om, of, os_,
+    ob_in, nb_in, steps_in, rate_in, g, end, om, of, os_,
     blocks, r2,
+    ob, nb, step_count, learning_rate,
     mine_g, raw, tail, olds, total, acode, right_code, left_code, scl, rscl, lscl,
     a_left, a_right, sa_left, sa_right, f_left, f_right, sf_left, sf_right,
     zsum, zsnd, zscl, zr, zs, both,
     stg, st, mat, new, wb, own, snd, zero,
-    in_s, own_g, raw_s, raw_r, a_s, a_r, as_s, as_r, f_s, f_r, fs_s, fs_r, zd_s, zd_r, zc_s, zc_r, gc_s, gc_r,
-    s1_s, s1_r, st_s, st_r, w1_s, w1_r, zu_s, zu_r, zd2_s, zd2_r, rt_s, rt_r, lf_s, lf_r,
+    sc_s, col_s, in_s, own_g, raw_s, raw_r, a_s, a_r, as_s, as_r, f_s, f_r, fs_s, fs_r, zd_s, zd_r, zc_s, zc_r, gc_s, gc_r,
+    s1_s, s1_r, st_s, st_r, w1_s, w1_r, zp_s, zp_r, zq_s, zq_r, xq_s, xq_r, rt_s, rt_r, lf_s, lf_r,
     rr_s, rr_r, rl_s, rl_r, cx_s, cx_r, s2_s, s2_r, own_s,
 ):
     node, y = lax.axis_index("node"), lax.axis_index("local")
@@ -79,15 +80,23 @@
 
     barrier = pltpu.get_barrier_semaphore()
 
-    def greet(d, carry):
-        pl.semaphore_signal(barrier, inc=1, device_id=(((chip + d) % CHIPS) * 2 + c, y), device_id_type=MESH)
-        return carry
-
-    lax.fori_loop(1, CHIPS, greet, 0)
-    pl.semaphore_signal(barrier, inc=1, device_id=(chip * 2 + 1 - c, y), device_id_type=MESH)
+    def greet(to_chip, to_core, to_y):
+        pl.semaphore_signal(barrier, inc=1, device_id=(to_chip * 2 + to_core, to_y), device_id_type=MESH)
+
+    greet(chip, 1 - c, y)
+    for d in range(1, NX):
+        greet((x + d) % NX * NZ + z, c, y)
+    for d in range(1, NZ):
+        greet(x * NZ + (z + d) % NZ, c, y)
     for d in range(1, NY):
-        pl.semaphore_signal(barrier, inc=1, device_id=(node, (y + d) % NY), device_id_type=MESH)
-
+        greet(chip, c, (y + d) % NY)
+
+    scalars = [
+        pltpu.make_async_copy(src, dst, sc_s.at[a])
+        for a, (src, dst) in enumerate(((ob_in, ob), (nb_in, nb), (steps_in, step_count), (rate_in, learning_rate)))
+    ]
+    for copy in scalars:
+        copy.start()
     state_in = [pltpu.make_async_copy(old.at[0], olds.at[a], in_s.at[a]) for a, old in enumerate((om, of, os_))]
     for copy in state_in:
         copy.start()
@@ -116,7 +125,7 @@
     for t in range(TILES, CHIPS):
         total[t] = jnp.zeros((HALF, LANE), F32)
 
-    pl.semaphore_wait(barrier, CHIPS - 1 + 1 + NY - 1)
+    pl.semaphore_wait(barrier, 1 + NX - 1 + NZ - 1 + NY - 1)
 
     @pl.when(c == 0)
     def _():
@@ -138,20 +147,8 @@
     def _():
         pltpu.make_async_copy(mine_g.at[0:224], mine_g.at[0:224], own_g).wait()
 
-    def state_out(d, carry):
-        to = (chip + d) % CHIPS
-
-        @pl.when(to < TILES)
-        def _():
-            send(stg.at[to], st.at[c, chip], s1_s, s1_r, to).start()
-
-        return carry
-
-    lax.fori_loop(1, CHIPS, state_out, 0)
-
-    @pl.when(chip < TILES)
-    def _():
-        pltpu.make_async_copy(stg.at[chip], st.at[c, chip], s1_r).start()
+    for d in range(1, NX):
+        pl.semaphore_signal(col_s, inc=1, device_id=(((x + d) % NX * NZ + z) * 2 + c, y), device_id_type=MESH)
 
     right_x, left_x, far_x = (x + 1) % NX, (x + 3) % NX, (x + 2) % NX
     right_chip, left_chip = right_x * NZ + z, left_x * NZ + z
@@ -239,15 +236,39 @@
     neighbours(0)
     pair(2)
     neighbours(1)
+
+    pl.semaphore_wait(col_s, NX - 1)
+
+    def state_out(d, carry):
+        to = (chip + d) % CHIPS
+
+        @pl.when(to < TILES)
+        def _():
+            send(stg.at[to], st.at[c, chip], s1_s, s1_r, to).start()
+
+        return carry
+
+    lax.fori_loop(1, CHIPS, state_out, 0)
+
+    @pl.when(chip < TILES)
+    def _():
+        pltpu.make_async_copy(stg.at[chip], st.at[c, chip], s1_r).start()
+
     along_z(0)
+    pair(3)
     neighbours(2)
+    along_z(1)
+    neighbours(3)
+    along_z(2)
 
     @pl.when(chip < TILES)
     def _():
         pltpu.make_async_copy(st.at[c], st.at[c], s1_r).wait()
 
     st_copy = start(send(st.at[c], st.at[c], st_s, st_r, chip, 1 - c))
-    along_z(1)
+    along_z(3)
+    for copy in scalars:
+        copy.wait()
 
     st_copy.wait_recv()
     for a in range(3):
@@ -262,7 +283,6 @@
         return i
 
     lax.fori_loop(0, SEGMENTS, place, jnp.int32(0))
-    along_z(2)
 
     gcopies = []
     for k, (first, rows) in enumerate(CHUNKS):
@@ -325,38 +345,36 @@
 
     for copy in w1:
         copy.wait_recv()
-    keep = pltpu.make_async_copy(own, blocks.at[c, chip], own_s)
+    keep = pltpu.make_async_copy(own, blocks.at[c, x, z], own_s)
     keep.start()
     up, down = x * NZ + (z + 1) % NZ, x * NZ + (z + NZ - 1) % NZ
-    right, left = ((x + 1) % NX) * NZ, ((x + 3) % NX) * NZ
-    across = ((x + 2) % NX) * NZ
+    three, low_rows, high_rows = slice(0, 3), slice(0, 32), slice(32, 64)
     from_left, from_right, relay_left, relay_right = [], [], [], []
-
-    def share(src, slot, e):
-        start(send(src, blocks.at[c, slot], cx_s.at[e], cx_r, chip, 1 - c))
-
-    def climb(src, slot, s, part=None):
-        dst = blocks.at[c, slot] if part is None else blocks.at[c, slot, part]
-        return start(send(src, dst, zu_s.at[s], zu_r.at[s], up))
-
-    def descend(src, slot, s, part=None):
-        dst = blocks.at[c, slot] if part is None else blocks.at[c, slot, part]
-        return start(send(src, dst, zd2_s.at[s], zd2_r.at[s], down))
-
-    def spread(src, slot, e):
-        from_left.append(start(send(src, blocks.at[c, slot], rt_s.at[e], rt_r.at[e], right + z)))
-        from_right.append(start(send(src, blocks.at[c, slot], lf_s.at[e], lf_r.at[e], left + z)))
-        share(src, slot, e)
+    shares = []
+
+    def share(src, dst):
+        shares.append(start(send(src, dst, cx_s.at[len(shares)], cx_r, chip, 1 - c)))
+
+    def pass_on(src, dst, sems, way, s):
+        return start(send(src, dst, sems[0].at[way, s], sems[1].at[way, s], (up, down)[way]))
+
+    def spread(src, at, e):
+        dst = blocks.at[c, x, at, three]
+        from_left.append(start(send(src, dst, rt_s.at[e], rt_r.at[e], right_chip)))
+        from_right.append(start(send(src, dst, lf_s.at[e], lf_r.at[e], left_chip)))
+        share(src, dst)
 
     def relay(at, e):
         from_left[e].wait_recv()
-        half = blocks.at[c, left + at, 0:2]
-        relay_left.append(start(send(half, half, rr_s.at[e], rr_r.at[e], right + z)))
-        share(blocks.at[c, left + at], left + at, 8 + e)
+        half = blocks.at[c, left_x, at, three, low_rows]
+        relay_left.append(start(send(half, half, rr_s.at[e], rr_r.at[e], right_chip)))
+        whole = blocks.at[c, left_x, at, three]
+        share(whole, whole)
         from_right[e].wait_recv()
-        half = blocks.at[c, right + at, 2:4]
-        relay_right.append(start(send(half, half, rl_s.at[e], rl_r.at[e], left + z)))
-        share(blocks.at[c, right + at], right + at, 16 + e)
+        half = blocks.at[c, right_x, at, three, high_rows]
+        relay_right.append(start(send(half, half, rl_s.at[e], rl_r.at[e], left_chip)))
+        whole = blocks.at[c, right_x, at, three]
+        share(whole, whole)
 
     owner = (48 - c - chip) % CHIPS
 
@@ -374,43 +392,66 @@
     def _():
         pltpu.make_async_copy(snd.at[owner], r2.at[chip], s2_r).start()
 
-    place_of = [z]
-    climbing, descending = climb(own, chip, 0), descend(own, chip, 0)
-    spread(own, chip, 0)
+    zp, zq = (zp_s, zp_r), (zq_s, zq_r)
+    places = [z]
+    climbing, descending = (pass_on(own.at[three], blocks.at[c, x, z, three], zp, way, 0) for way in range(2))
+    quarters = []
+    for d in range(1, NX):
+        to = (x + d) % NX * NZ + z
+        quarters.append(start(send(own.at[3], blocks.at[c, x, z, 3], xq_s.at[d - 1], xq_r.at[d - 1], to)))
+    spread(own.at[three], z, 0)
     lax.fori_loop(1, 8, owners_out, 0)
+    keep.wait()
+    for copy in quarters:
+        copy.wait_recv()
+    column = blocks.at[c, :, z, 3]
+    rising, sinking = (pass_on(column, column, zq, way, 0) for way in range(2))
+    share(column, column)
     for s in range(1, NZ // 2):
         low, high = (z + NZ - s) % NZ, (z + s) % NZ
+        final = s == NZ // 2 - 1
         climbing.wait_recv()
-        block = blocks.at[c, x * NZ + low]
-        if s < NZ // 2 - 1:
-            climbing = climb(block, x * NZ + low, s)
-        else:
-            climbing = climb(blocks.at[c, x * NZ + low, 0:2], x * NZ + low, s, slice(0, 2))
-        spread(block, x * NZ + low, 2 * s - 1)
+        block = blocks.at[c, x, low, three]
+        onward = blocks.at[c, x, low, three, low_rows] if final else block
+        climbing = pass_on(onward, onward, zp, 0, s)
+        spread(block, low, 2 * s - 1)
         descending.wait_recv()
-        block = blocks.at[c, x * NZ + high]
-        if s < NZ // 2 - 1:
-            descending = descend(block, x * NZ + high, s)
-        else:
-            descending = descend(blocks.at[c, x * NZ + high, 2:4], x * NZ + high, s, slice(2, 4))
-        spread(block, x * NZ + high, 2 * s)
-        for e in range(len(place_of) - (1 if s == 1 else 2), len(place_of)):
-            relay(place_of[e], e)
-        place_of += [low, high]
+        block = blocks.at[c, x, high, three]
+        onward = blocks.at[c, x, high, three, high_rows] if final else block
+        descending = pass_on(onward, onward, zp, 1, s)
+        spread(block, high, 2 * s)
+        rising.wait_recv()
+        column = blocks.at[c, :, low, 3]
+        onward = blocks.at[c, 0:2, low, 3] if final else column
+        rising = pass_on(onward, onward, zq, 0, s)
+        share(column, column)
+        sinking.wait_recv()
+        column = blocks.at[c, :, high, 3]
+        onward = blocks.at[c, 2:4, high, 3] if final else column
+        sinking = pass_on(onward, onward, zq, 1, s)
+        share(column, column)
+        for e in range(max(0, 2 * s - 3), 2 * s - 1):
+            relay(places[e], e)
+        places += [low, high]
         lax.fori_loop(8 * s, 8 * s + 8, owners_out, 0)
     climbing.wait_recv()
     descending.wait_recv()
     last = (z + NZ // 2) % NZ
-    spread(blocks.at[c, x * NZ + last], x * NZ + last, NZ - 1)
-    place_of.append(last)
+    spread(blocks.at[c, x, last, three], last, NZ - 1)
+    places.append(last)
+    rising.wait_recv()
+    sinking.wait_recv()
+    column = blocks.at[c, :, last, 3]
+    share(column, column)
 
     for e in range(NZ - 3, NZ):
-        relay(place_of[e], e)
+        relay(places[e], e)
+
     for e in range(NZ):
         relay_left[e].wait_recv()
         relay_right[e].wait_recv()
-        slot = across + place_of[e]
-        share(blocks.at[c, slot], slot, 24 + e)
+        whole = blocks.at[c, far_x, places[e], three]
+        share(whole, whole)
 
     @pl.when(owner < OWNERS // 2)
     def _():
@@ -431,7 +472,6 @@
     def _():
         pltpu.make_async_copy(snd.at[0:26], snd.at[0:26], s2_s).wait()
 
-    keep.wait()
     pltpu.make_async_copy(blocks.at[1 - c], blocks.at[1 - c], cx_r).wait()
     for k, (first, rows) in enumerate(CHUNKS):
         pltpu.make_async_copy(raw.at[first : first + rows], raw.at[first : first + rows], raw_s.at[k]).wait()
@@ -448,28 +488,49 @@
         copy.wait_send()
 
 
-def lay_out(blocks, r2, o_m, o_f, o_s, o_w):
-    q = pl.program_id(0)
+def lay_out(blocks, r2, o_m, o_f, o_s, o_w, got, rows, state, wide, in_s, out_s):
+    copies = [pltpu.make_async_copy(blocks.at[:, :, :, q], got.at[q], in_s.at[q]) for q in range(NY)]
+    copies.append(pltpu.make_async_copy(r2, rows, in_s.at[NY]))
+    for copy in copies:
+        copy.start()
+    outs = []
+
+    def out(src, dst):
+        outs.append(pltpu.make_async_copy(src, dst, out_s.at[len(outs)]))
+        outs[-1].start()
+
+    for q in range(NY):
+        copies[q].wait()
+        for t in range(TILES):
+            col = slice(t * LANE, (t + 1) * LANE)
+            wide[q, 0:64, col] = got[q, 0, t // NZ, t % NZ]
+            wide[q, 64:115, col] = got[q, 1, t // NZ, t % NZ, 0:51]
+        out(wide.at[q], o_w.at[:, q * WIDTH : (q + 1) * WIDTH])
+
+    copies[NY].wait()
 
     def tile(t, carry):
-        for a, out in enumerate((o_m, o_f, o_s)):
+        for a in range(3):
             for s in range(CAP_NEW):
-                out[s, t] = r2[t, CAP_NEW * a + s : CAP_NEW * a + s + 1]
+                state[a, s, t] = rows[t, CAP_NEW * a + s : CAP_NEW * a + s + 1]
         return carry
 
-    lax.fori_loop(8 * q, jnp.minimum(8 * q + 8, TILES), tile, 0)
-    for t in range(TILES):
-        col = slice(t * LANE, (t + 1) * LANE)
-        o_w[0:64, col] = blocks[0, t, 0]
-        o_w[64:115, col] = blocks[1, t, 0, 0:51]
+    lax.fori_loop(0, TILES, tile, 0)
+    for a, dst in enumerate((o_m, o_f, o_s)):
+        out(state.at[a], dst)
+    for copy in outs:
+        copy.wait()
 
 
 def on_device(grad_partials, old_master, old_first, old_second, old_bounds, new_bounds, step_count, learning_rate):
-    smem = pl.BlockSpec(memory_space=pltpu.SMEM)
     dma = pltpu.SemaphoreType.DMA
     hbm = pl.BlockSpec(memory_space=pl.ANY)
     scale = pltpu.VMEM((NC, 1, LANE), F32)
     scratch = [
+        pltpu.SMEM((NODES + 1,), I32),
+        pltpu.SMEM((OWNERS + 1,), I32),
+        pltpu.SMEM((1,), I32),
+        pltpu.SMEM((1,), F32),
         pltpu.VMEM((HALF, WIDTH), BF16),
         pltpu.VMEM((HALF, WIDTH), BF16),
         pltpu.VMEM((16, WIDTH), BF16),
@@ -499,6 +560,7 @@
         pltpu.VMEM((NY, PART, LANE), BF16),
         pltpu.VMEM((OWNERS // 2, 3 * CAP_NEW, LANE), F32),
         pltpu.VMEM((TILES, 3 * CAP_NEW, LANE), F32),
+        dma((4,)), pltpu.SemaphoreType.REGULAR,
         dma((3,)), dma,
         dma((NC,)), dma((NC,)),
         dma((2, NC)), dma((2, NC)), dma((2, NC)), dma((2, NC)),
@@ -508,13 +570,14 @@
         dma, dma,
         dma, dma,
         dma((NY - 1,)), dma((NY - 1,)),
-        dma((NZ // 2,)), dma((NZ // 2,)),
-        dma((NZ // 2,)), dma((NZ // 2,)),
+        dma((2, NZ // 2)), dma((2, NZ // 2)),
+        dma((2, NZ // 2)), dma((2, NZ // 2)),
+        dma((NX - 1,)), dma((NX - 1,)),
         dma((NZ,)), dma((NZ,)),
         dma((NZ,)), dma((NZ,)),
         dma((NZ,)), dma((NZ,)),
         dma((NZ,)), dma((NZ,)),
-        dma((CHIPS,)), dma,
+        dma((40,)), dma,
         dma, dma,
         dma,
     ]
@@ -522,27 +585,31 @@
         kernel,
         name="adamw_move",
         out_shape=(
-            jax.ShapeDtypeStruct((2, CHIPS, NY, PART, LANE), BF16),
+            jax.ShapeDtypeStruct((2, NX, NZ, NY, PART, LANE), BF16),
             jax.ShapeDtypeStruct((CHIPS, 3 * CAP_NEW, LANE), F32),
         ),
-        in_specs=[smem, smem, smem, smem, hbm, pl.BlockSpec((1, 16, WIDTH), lambda i: (0, 28, 0)), hbm, hbm, hbm],
+        in_specs=[hbm, hbm, hbm, hbm, hbm, pl.BlockSpec((1, 16, WIDTH), lambda i: (0, 28, 0)), hbm, hbm, hbm],
         grid=(1,),
         out_specs=(hbm, hbm),
         scratch_shapes=scratch,
         compiler_params=pltpu.CompilerParams(collective_id=0, has_side_effects=True, vmem_limit_bytes=56 * 2**20),
     )(old_bounds, new_bounds, step_count, learning_rate, grad_partials, grad_partials, old_master, old_first, old_second)
-    whole = pl.BlockSpec((CAP_NEW, TILES, 1, LANE), lambda q: (0, 0, 0, 0))
     rows = jax.ShapeDtypeStruct((CAP_NEW, TILES, 1, LANE), F32)
     outs = pl.pallas_call(
         lay_out,
         name="lay_out",
-        grid=(NY,),
         out_shape=(rows, rows, rows, jax.ShapeDtypeStruct((115, NY * WIDTH), BF16)),
-        in_specs=[
-            pl.BlockSpec((2, CHIPS, 1, PART, LANE), lambda q: (0, 0, q, 0, 0)),
-            pl.BlockSpec((CHIPS, 3 * CAP_NEW, LANE), lambda q: (0, 0, 0)),
+        in_specs=[hbm, hbm],
+        out_specs=(hbm, hbm, hbm, hbm),
+        scratch_shapes=[
+            pltpu.VMEM((NY, 2, NX, NZ, PART, LANE), BF16),
+            pltpu.VMEM((CHIPS, 3 * CAP_NEW, LANE), F32),
+            pltpu.VMEM((3, CAP_NEW, TILES, 1, LANE), F32),
+            pltpu.VMEM((NY, 115, WIDTH), BF16),
+            dma((NY + 1,)),
+            dma((NY + 3,)),
         ],
-        out_specs=(whole, whole, whole, pl.BlockSpec((115, WIDTH), lambda q: (0, q))),
+        compiler_params=pltpu.CompilerParams(vmem_limit_bytes=60 * 2**20),
     )(blocks, r2)
     return tuple(out.reshape(1, CAP_NEW, WIDTH) for out in outs[:3]) + (outs[3],)
 

time: 91 us -> 87.5 us (0.962)
  Pallas kernels: 88.8 us -> 85.4 us
    pallas_call x1, Pallas kernels: 83.5 us -> 81.5 us  [on_device(): pl.pallas_call(kernel, name='adamw_move', out_shape=(jax.ShapeDtypeStruct...]
    pallas_call x1, Pallas kernels: 5.33 us -> 3.88 us  [on_device(): pl.pallas_call(lay_out, name='lay_out', out_shape=(rows, rows, rows, jax....]
where the time goes in v3:
time: 87.5 us; the launch traced here: 87.3 us
  Pallas kernels  85.4 us (98%)
  between operations  1.93 us (2%)
    pallas_call x1, Pallas kernels, on_device(): pl.pallas_call(kernel, name='adamw_move', out_shape=(jax.ShapeDtypeStruct...  81.5 us
    pallas_call x1, Pallas kernels, on_device(): pl.pallas_call(lay_out, name='lay_out', out_shape=(rows, rows, rows, jax....  3.88 us

profile of v3, /device:TPU:1, one launch (start us, length us, event | category | flops | bytes accessed | tf_op | source)
XLA Modules:
  0.0 87.3 jit_solution(1813129689686494083)
XLA Ops:
  1.9 81.5 %adamw_move.1 = (bf16[2,4,8,4,64,128]{5,4,3,2,1,0:T(8,128)(2,1)}, f32[32,36,128]{2,1,0:T(8,128)}) custom-call(s32[65]{0:T(128)} %ob_in.1, s32[53]{0:T(128)} %nb_in.1, s32[1]{0:T(128)S(6)} %copy.15.steps_in, f32[1]{0:T(128)S(6)} %copy.16.rate_in, bf16[1,460,3712]{2,1,0:T(8,128)(2,1)} %end.1, bf16[1,460,3712]{2,1,0:T(8,128)(2,1)} %end.1, f32[1,8,3712]{2,1,0:T(8,128)} %om.1, ...), custom_call_target="tpu_custom_call" | custom-call | tf_op jit(solution)/shard_map/adamw_move/pallas_call | solution.py:584
  83.5 3.9 %lay_out.1 = (f32[12,29,1,128]{3,2,1,0:T(1,128)}, f32[12,29,1,128]{3,2,1,0:T(1,128)}, f32[12,29,1,128]{3,2,1,0:T(1,128)}, bf16[115,14848]{1,0:T(8,128)(2,1)}) custom-call(bf16[2,4,8,4,64,128]{5,4,3,2,1,0:T(8,128)(2,1)} %get-tuple-element.10.blocks, f32[32,36,128]{2,1,0:T(8,128)} %get-tuple-element.11.r2), custom_call_target="tpu_custom_call" | custom-call | tf_op jit(solution)/shard_map/lay_out/pallas_call | solution.py:598

commit v4 on v3

v4 whole, which is shorter than its diff:
```python
import jax
import jax.numpy as jnp
from jax import lax
from jax.experimental import pallas as pl
from jax.experimental.pallas import tpu as pltpu
from jax.sharding import PartitionSpec as P

MESH = pl.DeviceIdType.MESH
F32, BF16, I16, I32 = jnp.float32, jnp.bfloat16, jnp.int16, jnp.int32

UNITS = 460
WIDTH = 3712
LANE = 128
TILES = WIDTH // LANE
NODES = 64
CHIPS = 32
NX, NZ, NY = 4, 8, 4
HALF = 240
SECOND = 224
CHUNKS = ((0, 64), (64, 64), (128, 64), (192, 48))
NC = len(CHUNKS)
SEGMENTS = 115
CAP_NEW = 12
OWNERS = 52
PART = 64
LEVEL = 32760.0

beta_first = 0.9
beta_second = 0.95
adam_eps = 1e-08
decay = 0.1


def power(base, steps):
    result = jnp.float32(1.0)
    factor = float(base)
    for bit in range(5):
        result = jnp.where((steps // (1 << bit)) % 2 == 1, result * jnp.float32(factor), result)
        factor = factor * factor
    return result


def encode(value, inverse):
    return jnp.round(value * inverse).astype(I32).astype(I16)


def decode(code, scale):
    return code.astype(I32).astype(F32) * scale


def kernel(
    ob_in, nb_in, steps_in, rate_in, g, end, om, of, os_,
    blocks, r2,
    ob, nb, step_count, learning_rate,
    mine_g, raw, tail, olds, total, acode, right_code, left_code, scl, rscl, lscl, a_in, sa, f_in, sf,
    zsum, zsnd, zscl, zr, zs, grad,
    stg, st, mat, new, peer, wb, snd, zero,
    sc_s, col_s, in_s, own_g, raw_s, raw_r, a_s, a_r, as_s, as_r, f_s, f_r, fs_s, fs_r, zd_s, zd_r, zc_s, zc_r,
    s1_s, s1_r, st_s, st_r, ex_s, ex_r, w_s, w_r, x_s, x_r, far_s, far_r, cx_s, cx_r, s2_s, s2_r,
):
    node, y = lax.axis_index("node"), lax.axis_index("local")
    c, chip = node % 2, node // 2
    x, z = chip // NZ, chip % NZ

    def send(src, dst, ss, rs, to_chip, to_core=None, to_y=None):
        core = c if to_core is None else to_core
        return pltpu.make_async_remote_copy(
            src_ref=src, dst_ref=dst, send_sem=ss, recv_sem=rs,
            device_id=(to_chip * 2 + core, y if to_y is None else to_y), device_id_type=MESH,
        )

    def start(src, dst, ss, rs, to_chip, to_core=None, to_y=None):
        send(src, dst, ss, rs, to_chip, to_core, to_y).start()

    def arrived(ref, sem):
        pltpu.make_async_copy(ref, ref, sem).wait()

    barrier = pltpu.get_barrier_semaphore()

    def greet(to_chip, to_core, to_y):
        pl.semaphore_signal(barrier, inc=1, device_id=(to_chip * 2 + to_core, to_y), device_id_type=MESH)

    greet(chip, 1 - c, y)
    for d in range(1, NX):
        greet((x + d) % NX * NZ + z, c, y)
    for d in range(1, NZ):
        greet(x * NZ + (z + d) % NZ, c, y)
    for d in range(1, NY):
        greet(chip, c, (y + d) % NY)

    scalars = [
        pltpu.make_async_copy(src, dst, sc_s.at[a])
        for a, (src, dst) in enumerate(((ob_in, ob), (nb_in, nb), (steps_in, step_count), (rate_in, learning_rate)))
    ]
    for copy in scalars:
        copy.start()
    state_in = [pltpu.make_async_copy(old.at[0], olds.at[a], in_s.at[a]) for a, old in enumerate((om, of, os_))]
    for copy in state_in:
        copy.start()
    row = lax.broadcasted_iota(I32, (16, WIDTH), 0)
    tail[...] = jnp.where(row < 12, end[0].astype(F32), 0.0).astype(BF16)

    @pl.when(c == 0)
    def _():
        pltpu.make_async_copy(g.at[0, 0:HALF], mine_g, own_g).start()

    @pl.when(c == 1)
    def _():
        pltpu.make_async_copy(g.at[0, SECOND:448], mine_g.at[0:224], own_g).start()
        mine_g[224:240] = tail[...]

    for copy in state_in:
        copy.wait()

    def stage(t, carry):
        col = pl.ds(pl.multiple_of(t * LANE, LANE), LANE)
        for a in range(3):
            stg[t, a] = olds[a, :, col]
        return carry

    lax.fori_loop(0, TILES, stage, 0)
    for t in range(TILES, CHIPS):
        total[t] = jnp.zeros((HALF, LANE), F32)

    pl.semaphore_wait(barrier, 1 + NX - 1 + NZ - 1 + NY - 1)

    @pl.when(c == 0)
    def _():
        for k, (first, rows) in enumerate(CHUNKS):
            rows = min(rows, 224 - first)
            send(g.at[0, SECOND + first : SECOND + first + rows], raw.at[first : first + rows], raw_s.at[k], raw_r.at[k], chip, 1).start()
        send(tail, raw.at[224:240], raw_s.at[NC - 1], raw_r.at[NC - 1], chip, 1).start()

    @pl.when(c == 1)
    def _():
        for k, (first, rows) in enumerate(CHUNKS):
            send(g.at[0, first : first + rows], raw.at[first : first + rows], raw_s.at[k], raw_r.at[k], chip, 0).start()

    @pl.when(c == 0)
    def _():
        pltpu.make_async_copy(mine_g, mine_g, own_g).wait()

    @pl.when(c == 1)
    def _():
        pltpu.make_async_copy(mine_g.at[0:224], mine_g.at[0:224], own_g).wait()

    for d in range(1, NX):
        pl.semaphore_signal(col_s, inc=1, device_id=(((x + d) % NX * NZ + z) * 2 + c, y), device_id_type=MESH)

    right_x, left_x, far_x = (x + 1) % NX, (x + 3) % NX, (x + 2) % NX
    right_chip, left_chip = right_x * NZ + z, left_x * NZ + z

    def pair(k):
        first, rows = CHUNKS[k]
        at = slice(first, first + rows)
        arrived(raw.at[at], raw_r.at[k])

        def add(t, top):
            col = pl.ds(pl.multiple_of(t * LANE, LANE), LANE)
            value = mine_g[at, col].astype(F32) + raw[at, col].astype(F32)
            total[t, at] = value
            return jnp.maximum(top, jnp.abs(value))

        top = lax.fori_loop(0, TILES, add, jnp.zeros((rows, LANE), F32))
        top = jnp.maximum(jnp.max(top, axis=0, keepdims=True), 1e-30)
        scl[k] = top / LEVEL
        inverse = LEVEL / top

        def code(t, carry):
            acode[t, at] = encode(total[far_x * NZ + t, at], inverse)
            return carry

        lax.fori_loop(0, NZ, code, 0)
        start(acode.at[0:4, at], a_in.at[0, :, at], a_s, a_r.at[k], right_chip)
        start(acode.at[4:8, at], a_in.at[1, :, at], a_s, a_r.at[k], left_chip)
        start(scl.at[k], sa.at[0, k], as_s, as_r.at[k], right_chip)
        start(scl.at[k], sa.at[1, k], as_s, as_r.at[k], left_chip)

    def neighbours(k):
        first, rows = CHUNKS[k]
        at = slice(first, first + rows)
        arrived(a_in.at[:, :, at], a_r.at[k])
        arrived(sa.at[:, k], as_r.at[k])
        rscl[k] = scl[k] + sa[0, k]
        lscl[k] = scl[k] + sa[1, k]
        to_right, to_left = 1.0 / rscl[k], 1.0 / lscl[k]

        def code(t, carry):
            through = decode(a_in[0, t, at], sa[0, k])
            right_code[t, at] = encode(total[right_x * NZ + t, at] + through, to_right)
            right_code[t + 4, at] = encode(total[right_x * NZ + t + 4, at], to_right)
            through = decode(a_in[1, t, at], sa[1, k])
            left_code[t, at] = encode(total[left_x * NZ + t, at], to_left)
            left_code[t + 4, at] = encode(total[left_x * NZ + t + 4, at] + through, to_left)
            return carry

        lax.fori_loop(0, 4, code, 0)
        start(right_code.at[:, at], f_in.at[0, :, at], f_s, f_r.at[k], right_chip)
        start(left_code.at[:, at], f_in.at[1, :, at], f_s, f_r.at[k], left_chip)
        start(rscl.at[k], sf.at[0, k], fs_s, fs_r.at[k], right_chip)
        start(lscl.at[k], sf.at[1, k], fs_s, fs_r.at[k], left_chip)

    def along_z(k):
        first, rows = CHUNKS[k]
        at = slice(first, first + rows)
        arrived(f_in.at[:, :, at], f_r.at[k])
        arrived(sf.at[:, k], fs_r.at[k])
        zscl[k] = scl[k] + sf[0, k] + sf[1, k]
        inverse = 1.0 / zscl[k]

        def code(t, carry):
            value = total[x * NZ + t, at] + decode(f_in[0, t, at], sf[0, k]) + decode(f_in[1, t, at], sf[1, k])
            zsum[t, at] = value
            zsnd[t, at] = encode(value, inverse)
            return carry

        lax.fori_loop(0, NZ, code, 0)
        for d in range(1, NZ):
            gz = (z + d) % NZ
            to = x * NZ + gz
            start(zsnd.at[gz, at], zr.at[d - 1, at], zd_s, zd_r.at[k], to)
            start(zscl.at[k], zs.at[d - 1, k], zc_s, zc_r.at[k], to)

    pair(0)
    pair(1)
    neighbours(0)
    pair(2)
    neighbours(1)

    pl.semaphore_wait(col_s, NX - 1)

    def state_out(d, carry):
        to = (chip + d) % CHIPS

        @pl.when(to < TILES)
        def _():
            send(stg.at[to], st.at[c, chip], s1_s, s1_r, to).start()

        return carry

    lax.fori_loop(1, CHIPS, state_out, 0)

    @pl.when(chip < TILES)
    def _():
        pltpu.make_async_copy(stg.at[chip], st.at[c, chip], s1_r).start()

    along_z(0)
    pair(3)
    neighbours(2)
    along_z(1)
    neighbours(3)
    along_z(2)

    @pl.when(chip < TILES)
    def _():
        arrived(st.at[c], s1_r)

    start(st.at[c], st.at[c], st_s, st_r, chip, 1 - c)
    along_z(3)
    for copy in scalars:
        copy.wait()

    arrived(st.at[1 - c], st_r)
    for a in range(3):
        new[a, 464:480] = jnp.zeros((16, LANE), F32)

    def owner_of(s, i):
        return jnp.minimum(i + (ob[i + 1] <= 4 * s).astype(I32), NODES - 1)

    def place(s, i):
        i = owner_of(s, i)
        offset = jnp.clip(4 * s - ob[i], 0, 4)
        for a in range(3):
            mat[a, pl.ds(4 * s, 4)] = st[i % 2, i // 2, a, pl.ds(offset, 4)]
        return i

    before = lax.fori_loop(0, c * (SECOND // 4), owner_of, jnp.int32(0))
    lax.fori_loop(c * (SECOND // 4), c * (SECOND // 4) + HALF // 4, place, before)

    for k, (first, rows) in enumerate(CHUNKS):
        at = slice(first, first + rows)
        arrived(zr.at[:, at], zd_r.at[k])
        arrived(zs.at[:, k], zc_r.at[k])
        value = zsum[z, at]
        for d in range(NZ - 1):
            value = value + decode(zr[d, at], zs[d, k])
        grad[at] = value

    steps = step_count[0]
    rate = learning_rate[0]
    first_left = 1.0 - power(beta_first, steps)
    second_left = 1.0 - power(beta_second, steps)

    def step(b, carry):
        rows = pl.ds(pl.multiple_of(c * SECOND + b * 48, 16), 48)
        gradient = grad[pl.ds(pl.multiple_of(b * 48, 16), 48)]
        master = mat[0, rows]
        first_new = beta_first * mat[1, rows] + (1.0 - beta_first) * gradient
        second_new = beta_second * mat[2, rows] + (1.0 - beta_second) * gradient * gradient
        first_hat = first_new / first_left
        second_hat = second_new / second_left
        new[0, rows] = master - rate * (first_hat / (jnp.sqrt(second_hat) + adam_eps) + decay * master)
        new[1, rows] = first_new
        new[2, rows] = second_new
        return carry

    lax.fori_loop(0, HALF // 48, step, 0)

    for i in range(2):
        rows = new[0, pl.ds(c * 230 + 115 * i, 120)]
        wb[i] = jnp.concatenate([rows, jnp.zeros((8, LANE), F32)], axis=0).astype(BF16)
    for dz in (0, 4, 1, 7, 2, 6, 3, 5):
        for i in range(2):
            yy = 2 * c + i
            to = x * NZ + (z + dz) % NZ
            for other in range(2):
                core = (c + other) % 2
                src = wb.at[i, pl.ds(pl.multiple_of(core * PART, PART), PART)]
                dst = blocks.at[core, x, z, y]
                if dz == 0 and other == 0:
                    @pl.when(yy == y)
                    def _():
                        pltpu.make_async_copy(src, dst, w_r.at[0]).start()

                    @pl.when(yy != y)
                    def _():
                        start(src, dst, w_s, w_r.at[0], to, core, yy)
                else:
                    start(src, dst, w_s, w_r.at[dz], to, core, yy)

    @pl.when(c == 0)
    def _():
        send(new.at[:, 0:224], peer, ex_s, ex_r, chip, 1).start()

    @pl.when(c == 1)
    def _():
        send(new.at[:, 240:464], peer, ex_s, ex_r, chip, 0).start()

    arrived(peer, ex_r)
    theirs = pl.ds(pl.multiple_of((1 - c) * HALF, 16), 224)
    for a in range(3):
        new[a, theirs] = peer[a]

    def pick(m, carry):
        begin = jnp.clip(nb[2 * m + c], 0, UNITS)
        count = nb[2 * m + c + 1] - begin
        slot = lax.broadcasted_iota(I32, (CAP_NEW, LANE), 0)
        for a in range(3):
            rows = new[a, pl.ds(begin, CAP_NEW)]
            snd[m, CAP_NEW * a : CAP_NEW * (a + 1)] = jnp.where(slot < count, rows, 0.0)
        return carry

    lax.fori_loop(0, OWNERS // 2, pick, 0)

    def share(ref):
        start(ref, ref, cx_s, cx_r, chip, 1 - c)

    def spread(at, e):
        ref = blocks.at[c, x, at]
        start(ref, ref, x_s, x_r.at[0, e], right_chip)
        start(ref, ref, x_s, x_r.at[1, e], left_chip)
        share(ref)

    def relay(at, e):
        arrived(blocks.at[c, left_x, at], x_r.at[0, e])
        half = blocks.at[c, left_x, at, 0:2]
        start(half, half, far_s, far_r.at[e], right_chip)
        arrived(blocks.at[c, right_x, at], x_r.at[1, e])
        half = blocks.at[c, right_x, at, 2:4]
        start(half, half, far_s, far_r.at[e], left_chip)
        share(blocks.at[c, left_x, at])
        share(blocks.at[c, right_x, at])

    owner = (48 - c - chip) % CHIPS

    def owners_out(d, carry):
        to = (chip + d) % CHIPS
        m = (48 - c - to) % CHIPS

        @pl.when((m < OWNERS // 2) & (chip < TILES))
        def _():
            send(snd.at[m], r2.at[chip], s2_s, s2_r, to).start()

        return carry

    @pl.when((owner < OWNERS // 2) & (chip < TILES))
    def _():
        pltpu.make_async_copy(snd.at[owner], r2.at[chip], s2_r).start()

    order = (0, 1, 7, 2, 6, 3, 5, 4)
    for n, dz in enumerate(order):
        at = (z + NZ - dz) % NZ
        arrived(blocks.at[c, x, at], w_r.at[dz])
        spread(at, dz)
        if n >= 2:
            relay((z + NZ - order[n - 2]) % NZ, order[n - 2])
        if n >= 4:
            lax.fori_loop(max(8 * (n - 4), 1), 8 * (n - 4) + 8, owners_out, 0)

    for dz in order[6:]:
        relay((z + NZ - dz) % NZ, dz)

    for dz in order:
        ref = blocks.at[c, far_x, (z + NZ - dz) % NZ]
        arrived(ref, far_r.at[dz])
        share(ref)

    @pl.when(owner < OWNERS // 2)
    def _():
        arrived(r2.at[0:TILES], s2_r)

    @pl.when(owner >= OWNERS // 2)
    def _():
        zero[...] = jnp.zeros_like(zero)
        clear = pltpu.make_async_copy(zero, r2.at[0:TILES], s2_r)
        clear.start()
        clear.wait()

    @pl.when((owner < OWNERS // 2) & (chip < TILES))
    def _():
        arrived(snd.at[0:25], s2_s)

    @pl.when((owner >= OWNERS // 2) & (chip < TILES))
    def _():
        arrived(snd.at[0:26], s2_s)

    arrived(blocks.at[1 - c], cx_r)
    for k, (first, rows) in enumerate(CHUNKS):
        arrived(raw.at[first : first + rows], raw_s.at[k])

    @pl.when(chip < TILES)
    def _():
        arrived(stg.at[0:28], s1_s)

    @pl.when(chip >= TILES)
    def _():
        arrived(stg.at[0:29], s1_s)

    @pl.when(y // 2 != c)
    def _():
        arrived(blocks.at[c, 0], w_s)

    @pl.when(y // 2 == c)
    def _():
        arrived(total.at[0:31, 0:32], w_s)

    for ref, sem in (
        (acode, a_s), (sa, as_s), (f_in, f_s), (sf, fs_s), (zr, zd_s), (zs, zc_s), (st.at[c], st_s),
        (peer, ex_s), (blocks.at[c, 0:2], x_s), (blocks.at[c, 0], far_s), (blocks.at[c], cx_s),
    ):
        arrived(ref, sem)


def lay_out(blocks, r2, o_m, o_f, o_s, o_w, got, rows, state, wide, in_s, out_s):
    copies = [pltpu.make_async_copy(blocks.at[:, :, :, q], got.at[q], in_s.at[q]) for q in range(NY)]
    copies.append(pltpu.make_async_copy(r2, rows, in_s.at[NY]))
    for copy in copies:
        copy.start()
    outs = []

    def out(src, dst):
        outs.append(pltpu.make_async_copy(src, dst, out_s.at[len(outs)]))
        outs[-1].start()

    for q in range(NY):
        copies[q].wait()
        for t in range(TILES):
            col = slice(t * LANE, (t + 1) * LANE)
            wide[q, 0:64, col] = got[q, 0, t // NZ, t % NZ]
            wide[q, 64:115, col] = got[q, 1, t // NZ, t % NZ, 0:51]
        out(wide.at[q], o_w.at[:, q * WIDTH : (q + 1) * WIDTH])

    copies[NY].wait()

    def tile(t, carry):
        for a in range(3):
            for s in range(CAP_NEW):
                state[a, s, t] = rows[t, CAP_NEW * a + s : CAP_NEW * a + s + 1]
        return carry

    lax.fori_loop(0, TILES, tile, 0)
    for a, dst in enumerate((o_m, o_f, o_s)):
        out(state.at[a], dst)
    for copy in outs:
        copy.wait()


def on_device(grad_partials, old_master, old_first, old_second, old_bounds, new_bounds, step_count, learning_rate):
    dma = pltpu.SemaphoreType.DMA
    hbm = pl.BlockSpec(memory_space=pl.ANY)
    scale = pltpu.VMEM((NC, 1, LANE), F32)
    scratch = [
        pltpu.SMEM((NODES + 1,), I32),
        pltpu.SMEM((OWNERS + 1,), I32),
        pltpu.SMEM((1,), I32),
        pltpu.SMEM((1,), F32),
        pltpu.VMEM((HALF, WIDTH), BF16),
        pltpu.VMEM((HALF, WIDTH), BF16),
        pltpu.VMEM((16, WIDTH), BF16),
        pltpu.VMEM((3, 8, WIDTH), F32),
        pltpu.VMEM((CHIPS, HALF, LANE), F32),
        pltpu.VMEM((NZ, HALF, LANE), I16),
        pltpu.VMEM((NZ, HALF, LANE), I16),
        pltpu.VMEM((NZ, HALF, LANE), I16),
        scale, scale, scale,
        pltpu.VMEM((2, NZ // 2, HALF, LANE), I16),
        pltpu.VMEM((2, NC, 1, LANE), F32),
        pltpu.VMEM((2, NZ, HALF, LANE), I16),
        pltpu.VMEM((2, NC, 1, LANE), F32),
        pltpu.VMEM((NZ, HALF, LANE), F32),
        pltpu.VMEM((NZ, HALF, LANE), I16),
        scale,
        pltpu.VMEM((NZ - 1, HALF, LANE), I16),
        pltpu.VMEM((NZ - 1, NC, 1, LANE), F32),
        pltpu.VMEM((HALF, LANE), F32),
        pltpu.VMEM((CHIPS, 3, 8, LANE), F32),
        pltpu.VMEM((2, CHIPS, 3, 8, LANE), F32),
        pltpu.VMEM((3, 480, LANE), F32),
        pltpu.VMEM((3, 480, LANE), F32),
        pltpu.VMEM((3, 224, LANE), F32),
        pltpu.VMEM((2, 128, LANE), BF16),
        pltpu.VMEM((OWNERS // 2, 3 * CAP_NEW, LANE), F32),
        pltpu.VMEM((TILES, 3 * CAP_NEW, LANE), F32),
        dma((4,)), pltpu.SemaphoreType.REGULAR,
        dma((3,)), dma,
        dma((NC,)), dma((NC,)),
        dma, dma((NC,)), dma, dma((NC,)), dma, dma((NC,)), dma, dma((NC,)),
        dma, dma((NC,)), dma, dma((NC,)),
        dma, dma, dma, dma, dma, dma,
        dma, dma((NZ,)), dma, dma((2, NZ)), dma, dma((NZ,)), dma, dma,
        dma, dma,
    ]
    blocks, r2 = pl.pallas_call(
        kernel,
        name="adamw_move",
        out_shape=(
            jax.ShapeDtypeStruct((2, NX, NZ, NY, PART, LANE), BF16),
            jax.ShapeDtypeStruct((CHIPS, 3 * CAP_NEW, LANE), F32),
        ),
        in_specs=[hbm, hbm, hbm, hbm, hbm, pl.BlockSpec((1, 16, WIDTH), lambda i: (0, 28, 0)), hbm, hbm, hbm],
        grid=(1,),
        out_specs=(hbm, hbm),
        scratch_shapes=scratch,
        compiler_params=pltpu.CompilerParams(collective_id=0, has_side_effects=True, vmem_limit_bytes=56 * 2**20),
    )(old_bounds, new_bounds, step_count, learning_rate, grad_partials, grad_partials, old_master, old_first, old_second)
    rows = jax.ShapeDtypeStruct((CAP_NEW, TILES, 1, LANE), F32)
    outs = pl.pallas_call(
        lay_out,
        name="lay_out",
        out_shape=(rows, rows, rows, jax.ShapeDtypeStruct((115, NY * WIDTH), BF16)),
        in_specs=[hbm, hbm],
        out_specs=(hbm, hbm, hbm, hbm),
        scratch_shapes=[
            pltpu.VMEM((NY, 2, NX, NZ, PART, LANE), BF16),
            pltpu.VMEM((CHIPS, 3 * CAP_NEW, LANE), F32),
            pltpu.VMEM((3, CAP_NEW, TILES, 1, LANE), F32),
            pltpu.VMEM((NY, 115, WIDTH), BF16),
            dma((NY + 1,)),
            dma((NY + 3,)),
        ],
        compiler_params=pltpu.CompilerParams(vmem_limit_bytes=60 * 2**20),
    )(blocks, r2)
    return tuple(out.reshape(1, CAP_NEW, WIDTH) for out in outs[:3]) + (outs[3],)


def solution(mesh):
    split = P("node", None, "local")
    return jax.shard_map(
        on_device,
        mesh=mesh,
        in_specs=(split, split, split, split, P(), P(), P(), P()),
        out_specs=(split, split, split, P("local", None)),
        check_vma=False,
    )
```

time: 87.5 us -> 85.7 us (0.979)
  Pallas kernels: 85.4 us -> 83.1 us
    pallas_call x1, Pallas kernels: 81.5 us -> 79.3 us  [on_device(): pl.pallas_call(kernel, name='adamw_move', out_shape=(jax.ShapeDtypeStruct...]
where the time goes in v4:
time: 85.7 us; the launch traced here: 85.1 us
  Pallas kernels  83.1 us (97%)
  between operations  1.93 us (2%)
    pallas_call x1, Pallas kernels, on_device(): pl.pallas_call(kernel, name='adamw_move', out_shape=(jax.ShapeDtypeStruct...  79.3 us
    pallas_call x1, Pallas kernels, on_device(): pl.pallas_call(lay_out, name='lay_out', out_shape=(rows, rows, rows, jax....  3.88 us

profile of v4, /device:TPU:1, one launch (start us, length us, event | category | flops | bytes accessed | tf_op | source)
XLA Modules:
  0.0 85.1 jit_solution(7034695864991914261)
XLA Ops:
  1.9 79.3 %adamw_move.1 = (bf16[2,4,8,4,64,128]{5,4,3,2,1,0:T(8,128)(2,1)}, f32[32,36,128]{2,1,0:T(8,128)}) custom-call(s32[65]{0:T(128)} %ob_in.1, s32[53]{0:T(128)} %nb_in.1, s32[1]{0:T(128)S(6)} %copy.15.steps_in, f32[1]{0:T(128)S(6)} %copy.16.rate_in, bf16[1,460,3712]{2,1,0:T(8,128)(2,1)} %end.1, bf16[1,460,3712]{2,1,0:T(8,128)(2,1)} %end.1, f32[1,8,3712]{2,1,0:T(8,128)} %om.1, ...), custom_call_target="tpu_custom_call" | custom-call | tf_op jit(solution)/shard_map/adamw_move/pallas_call | solution.py:533
  81.2 3.9 %lay_out.1 = (f32[12,29,1,128]{3,2,1,0:T(1,128)}, f32[12,29,1,128]{3,2,1,0:T(1,128)}, f32[12,29,1,128]{3,2,1,0:T(1,128)}, bf16[115,14848]{1,0:T(8,128)(2,1)}) custom-call(bf16[2,4,8,4,64,128]{5,4,3,2,1,0:T(8,128)(2,1)} %get-tuple-element.10.blocks, f32[32,36,128]{2,1,0:T(8,128)} %get-tuple-element.11.r2), custom_call_target="tpu_custom_call" | custom-call | tf_op jit(solution)/shard_map/lay_out/pallas_call | solution.py:547

commit v5 on v4

--- a/solution.py
+++ b/solution.py
@@ -394,8 +394,8 @@
         spread(at, dz)
         if n >= 2:
             relay((z + NZ - order[n - 2]) % NZ, order[n - 2])
-        if n >= 4:
-            lax.fori_loop(max(8 * (n - 4), 1), 8 * (n - 4) + 8, owners_out, 0)
+        if n == 0:
+            lax.fori_loop(1, 32, owners_out, 0)
 
     for dz in order[6:]:
         relay((z + NZ - dz) % NZ, dz)

time: 85.7 us -> 83.1 us (0.970)
  Pallas kernels: 83.1 us -> 80.7 us
    pallas_call x1, Pallas kernels: 79.3 us -> 76.8 us  [on_device(): pl.pallas_call(kernel, name='adamw_move', out_shape=(jax.ShapeDtypeStruct...]
where the time goes in v5:
time: 83.1 us; the launch traced here: 82.6 us
  Pallas kernels  80.7 us (97%)
  between operations  1.93 us (2%)
    pallas_call x1, Pallas kernels, on_device(): pl.pallas_call(kernel, name='adamw_move', out_shape=(jax.ShapeDtypeStruct...  76.8 us
    pallas_call x1, Pallas kernels, on_device(): pl.pallas_call(lay_out, name='lay_out', out_shape=(rows, rows, rows, jax....  3.88 us

profile of v5, /device:TPU:1, one launch (start us, length us, event | category | flops | bytes accessed | tf_op | source)
XLA Modules:
  0.0 82.6 jit_solution(3729340359701473321)
XLA Ops:
  1.9 76.8 %adamw_move.1 = (bf16[2,4,8,4,64,128]{5,4,3,2,1,0:T(8,128)(2,1)}, f32[32,36,128]{2,1,0:T(8,128)}) custom-call(s32[65]{0:T(128)} %ob_in.1, s32[53]{0:T(128)} %nb_in.1, s32[1]{0:T(128)S(6)} %copy.15.steps_in, f32[1]{0:T(128)S(6)} %copy.16.rate_in, bf16[1,460,3712]{2,1,0:T(8,128)(2,1)} %end.1, bf16[1,460,3712]{2,1,0:T(8,128)(2,1)} %end.1, f32[1,8,3712]{2,1,0:T(8,128)} %om.1, ...), custom_call_target="tpu_custom_call" | custom-call | tf_op jit(solution)/shard_map/adamw_move/pallas_call | solution.py:533
  78.7 3.9 %lay_out.1 = (f32[12,29,1,128]{3,2,1,0:T(1,128)}, f32[12,29,1,128]{3,2,1,0:T(1,128)}, f32[12,29,1,128]{3,2,1,0:T(1,128)}, bf16[115,14848]{1,0:T(8,128)(2,1)}) custom-call(bf16[2,4,8,4,64,128]{5,4,3,2,1,0:T(8,128)(2,1)} %get-tuple-element.10.blocks, f32[32,36,128]{2,1,0:T(8,128)} %get-tuple-element.11.r2), custom_call_target="tpu_custom_call" | custom-call | tf_op jit(solution)/shard_map/lay_out/pallas_call | solution.py:547

commit v6 on v5

--- a/solution.py
+++ b/solution.py
@@ -147,6 +147,23 @@
     for d in range(1, NX):
         pl.semaphore_signal(col_s, inc=1, device_id=(((x + d) % NX * NZ + z) * 2 + c, y), device_id_type=MESH)
 
+    pl.semaphore_wait(col_s, NX - 1)
+
+    def state_out(d, carry):
+        to = (chip + d) % CHIPS
+
+        @pl.when(to < TILES)
+        def _():
+            send(stg.at[to], st.at[c, chip], s1_s, s1_r, to).start()
+
+        return carry
+
+    lax.fori_loop(1, CHIPS, state_out, 0)
+
+    @pl.when(chip < TILES)
+    def _():
+        pltpu.make_async_copy(stg.at[chip], st.at[c, chip], s1_r).start()
+
     right_x, left_x, far_x = (x + 1) % NX, (x + 3) % NX, (x + 2) % NX
     right_chip, left_chip = right_x * NZ + z, left_x * NZ + z
 
@@ -226,23 +243,6 @@
     neighbours(0)
     pair(2)
     neighbours(1)
-
-    pl.semaphore_wait(col_s, NX - 1)
-
-    def state_out(d, carry):
-        to = (chip + d) % CHIPS
-
-        @pl.when(to < TILES)
-        def _():
-            send(stg.at[to], st.at[c, chip], s1_s, s1_r, to).start()
-
-        return carry
-
-    lax.fori_loop(1, CHIPS, state_out, 0)
-
-    @pl.when(chip < TILES)
-    def _():
-        pltpu.make_async_copy(stg.at[chip], st.at[c, chip], s1_r).start()
 
     along_z(0)
     pair(3)
@@ -309,7 +309,7 @@
     for i in range(2):
         rows = new[0, pl.ds(c * 230 + 115 * i, 120)]
         wb[i] = jnp.concatenate([rows, jnp.zeros((8, LANE), F32)], axis=0).astype(BF16)
-    for dz in (0, 4, 1, 7, 2, 6, 3, 5):
+    for dz in (0, 1, 7, 2, 6, 3, 5, 4):
         for i in range(2):
             yy = 2 * c + i
             to = x * NZ + (z + dz) % NZ
@@ -387,6 +387,8 @@
     def _():
         pltpu.make_async_copy(snd.at[owner], r2.at[chip], s2_r).start()
 
+    lax.fori_loop(1, CHIPS, owners_out, 0)
+
     order = (0, 1, 7, 2, 6, 3, 5, 4)
     for n, dz in enumerate(order):
         at = (z + NZ - dz) % NZ
@@ -394,8 +396,6 @@
         spread(at, dz)
         if n >= 2:
             relay((z + NZ - order[n - 2]) % NZ, order[n - 2])
-        if n == 0:
-            lax.fori_loop(1, 32, owners_out, 0)
 
     for dz in order[6:]:
         relay((z + NZ - dz) % NZ, dz)

time: 83.1 us -> 80.7 us (0.971)
  Pallas kernels: 80.7 us -> 78.6 us
    pallas_call x1, Pallas kernels: 76.8 us -> 74.7 us  [on_device(): pl.pallas_call(kernel, name='adamw_move', out_shape=(jax.ShapeDtypeStruct...]
where the time goes in v6:
time: 80.7 us; the launch traced here: 80.5 us
  Pallas kernels  78.6 us (97%)
  between operations  1.93 us (2%)
    pallas_call x1, Pallas kernels, on_device(): pl.pallas_call(kernel, name='adamw_move', out_shape=(jax.ShapeDtypeStruct...  74.7 us
    pallas_call x1, Pallas kernels, on_device(): pl.pallas_call(lay_out, name='lay_out', out_shape=(rows, rows, rows, jax....  3.88 us

profile of v6, /device:TPU:1, one launch (start us, length us, event | category | flops | bytes accessed | tf_op | source)
XLA Modules:
  0.0 80.5 jit_solution(3783030359438619661)
XLA Ops:
  1.9 74.7 %adamw_move.1 = (bf16[2,4,8,4,64,128]{5,4,3,2,1,0:T(8,128)(2,1)}, f32[32,36,128]{2,1,0:T(8,128)}) custom-call(s32[65]{0:T(128)} %ob_in.1, s32[53]{0:T(128)} %nb_in.1, s32[1]{0:T(128)S(6)} %copy.15.steps_in, f32[1]{0:T(128)S(6)} %copy.16.rate_in, bf16[1,460,3712]{2,1,0:T(8,128)(2,1)} %end.1, bf16[1,460,3712]{2,1,0:T(8,128)(2,1)} %end.1, f32[1,8,3712]{2,1,0:T(8,128)} %om.1, ...), custom_call_target="tpu_custom_call" | custom-call | tf_op jit(solution)/shard_map/adamw_move/pallas_call | solution.py:533
  76.6 3.9 %lay_out.1 = (f32[12,29,1,128]{3,2,1,0:T(1,128)}, f32[12,29,1,128]{3,2,1,0:T(1,128)}, f32[12,29,1,128]{3,2,1,0:T(1,128)}, bf16[115,14848]{1,0:T(8,128)(2,1)}) custom-call(bf16[2,4,8,4,64,128]{5,4,3,2,1,0:T(8,128)(2,1)} %get-tuple-element.10.blocks, f32[32,36,128]{2,1,0:T(8,128)} %get-tuple-element.11.r2), custom_call_target="tpu_custom_call" | custom-call | tf_op jit(solution)/shard_map/lay_out/pallas_call | solution.py:547

commit v7 on v6

--- a/solution.py
+++ b/solution.py
@@ -452,8 +452,9 @@
 
 
 def lay_out(blocks, r2, o_m, o_f, o_s, o_w, got, rows, state, wide, in_s, out_s):
+    here = pltpu.make_async_copy(r2, rows, in_s.at[NY])
+    here.start()
     copies = [pltpu.make_async_copy(blocks.at[:, :, :, q], got.at[q], in_s.at[q]) for q in range(NY)]
-    copies.append(pltpu.make_async_copy(r2, rows, in_s.at[NY]))
     for copy in copies:
         copy.start()
     outs = []
@@ -462,6 +463,17 @@
         outs.append(pltpu.make_async_copy(src, dst, out_s.at[len(outs)]))
         outs[-1].start()
 
+    here.wait()
+
+    def tile(t, carry):
+        for a in range(3):
+            for s in range(CAP_NEW):
+                state[a, s, t] = rows[t, CAP_NEW * a + s : CAP_NEW * a + s + 1]
+        return carry
+
+    lax.fori_loop(0, TILES, tile, 0)
+    for a, dst in enumerate((o_m, o_f, o_s)):
+        out(state.at[a], dst)
     for q in range(NY):
         copies[q].wait()
         for t in range(TILES):
@@ -469,18 +481,6 @@
             wide[q, 0:64, col] = got[q, 0, t // NZ, t % NZ]
             wide[q, 64:115, col] = got[q, 1, t // NZ, t % NZ, 0:51]
         out(wide.at[q], o_w.at[:, q * WIDTH : (q + 1) * WIDTH])
-
-    copies[NY].wait()
-
-    def tile(t, carry):
-        for a in range(3):
-            for s in range(CAP_NEW):
-                state[a, s, t] = rows[t, CAP_NEW * a + s : CAP_NEW * a + s + 1]
-        return carry
-
-    lax.fori_loop(0, TILES, tile, 0)
-    for a, dst in enumerate((o_m, o_f, o_s)):
-        out(state.at[a], dst)
     for copy in outs:
         copy.wait()
 

time: 80.7 us -> 80.4 us (level)
  no operation moved by 1% of the time
where the time goes in v7:
time: 80.4 us; the launch traced here: 80.3 us
  Pallas kernels  78.3 us (97%)
  between operations  1.93 us (2%)
    pallas_call x1, Pallas kernels, on_device(): pl.pallas_call(kernel, name='adamw_move', out_shape=(jax.ShapeDtypeStruct...  74.7 us
    pallas_call x1, Pallas kernels, on_device(): pl.pallas_call(lay_out, name='lay_out', out_shape=(rows, rows, rows, jax....  3.63 us

profile of v7, /device:TPU:1, one launch (start us, length us, event | category | flops | bytes accessed | tf_op | source)
XLA Modules:
  0.0 80.3 jit_solution(8491592148944385497)
XLA Ops:
  1.9 74.7 %adamw_move.1 = (bf16[2,4,8,4,64,128]{5,4,3,2,1,0:T(8,128)(2,1)}, f32[32,36,128]{2,1,0:T(8,128)}) custom-call(s32[65]{0:T(128)} %ob_in.1, s32[53]{0:T(128)} %nb_in.1, s32[1]{0:T(128)S(6)} %copy.15.steps_in, f32[1]{0:T(128)S(6)} %copy.16.rate_in, bf16[1,460,3712]{2,1,0:T(8,128)(2,1)} %end.1, bf16[1,460,3712]{2,1,0:T(8,128)(2,1)} %end.1, f32[1,8,3712]{2,1,0:T(8,128)} %om.1, ...), custom_call_target="tpu_custom_call" | custom-call | tf_op jit(solution)/shard_map/adamw_move/pallas_call | solution.py:533
  76.6 3.6 %lay_out.1 = (f32[12,29,1,128]{3,2,1,0:T(1,128)}, f32[12,29,1,128]{3,2,1,0:T(1,128)}, f32[12,29,1,128]{3,2,1,0:T(1,128)}, bf16[115,14848]{1,0:T(8,128)(2,1)}) custom-call(bf16[2,4,8,4,64,128]{5,4,3,2,1,0:T(8,128)(2,1)} %get-tuple-element.10.blocks, f32[32,36,128]{2,1,0:T(8,128)} %get-tuple-element.11.r2), custom_call_target="tpu_custom_call" | custom-call | tf_op jit(solution)/shard_map/lay_out/pallas_call | solution.py:547

commit v8 on v7

--- a/solution.py
+++ b/solution.py
@@ -232,7 +232,7 @@
             return carry
 
         lax.fori_loop(0, NZ, code, 0)
-        for d in range(1, NZ):
+        for d in (1, 7, 2, 6, 3, 5, 4):
             gz = (z + d) % NZ
             to = x * NZ + gz
             start(zsnd.at[gz, at], zr.at[d - 1, at], zd_s, zd_r.at[k], to)

time: 80.4 us -> 80.4 us (level)
  no operation moved by 1% of the time
where the time goes in v8:
time: 80.4 us; the launch traced here: 80.3 us
  Pallas kernels  78.3 us (97%)
  between operations  1.93 us (2%)
    pallas_call x1, Pallas kernels, on_device(): pl.pallas_call(kernel, name='adamw_move', out_shape=(jax.ShapeDtypeStruct...  74.7 us
    pallas_call x1, Pallas kernels, on_device(): pl.pallas_call(lay_out, name='lay_out', out_shape=(rows, rows, rows, jax....  3.63 us

profile of v8, /device:TPU:1, one launch (start us, length us, event | category | flops | bytes accessed | tf_op | source)
XLA Modules:
  0.0 80.3 jit_solution(6027642949518074295)
XLA Ops:
  1.9 74.7 %adamw_move.1 = (bf16[2,4,8,4,64,128]{5,4,3,2,1,0:T(8,128)(2,1)}, f32[32,36,128]{2,1,0:T(8,128)}) custom-call(s32[65]{0:T(128)} %ob_in.1, s32[53]{0:T(128)} %nb_in.1, s32[1]{0:T(128)S(6)} %copy.15.steps_in, f32[1]{0:T(128)S(6)} %copy.16.rate_in, bf16[1,460,3712]{2,1,0:T(8,128)(2,1)} %end.1, bf16[1,460,3712]{2,1,0:T(8,128)(2,1)} %end.1, f32[1,8,3712]{2,1,0:T(8,128)} %om.1, ...), custom_call_target="tpu_custom_call" | custom-call | tf_op jit(solution)/shard_map/adamw_move/pallas_call | solution.py:533
  76.6 3.6 %lay_out.1 = (f32[12,29,1,128]{3,2,1,0:T(1,128)}, f32[12,29,1,128]{3,2,1,0:T(1,128)}, f32[12,29,1,128]{3,2,1,0:T(1,128)}, bf16[115,14848]{1,0:T(8,128)(2,1)}) custom-call(bf16[2,4,8,4,64,128]{5,4,3,2,1,0:T(8,128)(2,1)} %get-tuple-element.10.blocks, f32[32,36,128]{2,1,0:T(8,128)} %get-tuple-element.11.r2), custom_call_target="tpu_custom_call" | custom-call | tf_op jit(solution)/shard_map/lay_out/pallas_call | solution.py:547
